TPU v7x, 256 devices: a whole 4x4x8 slice. The times are simulated.
256 devices in a mesh: slab: 16 (over y_lo, z), fsdp: 16 (over x, y_hi, core).
Axes of the slice: x: 4, y: 4 (y_hi: 2, y_lo: 2; y = y_hi * 2 + y_lo), z: 8, core: 2. Of those that a mesh axis runs over, the one named last changes fastest.
Arguments:
- hidden: bfloat16 [6144, 3072], P('slab'), may hold values from -6 to 6
- noise: bfloat16 [6144, 3072], P('slab', 'fsdp'), may hold values from -6 to 6
- norm_gain: float32 [3072], replicated, may hold values from 0.5 to 1.5
- qk_gain: float32 [2, 128], replicated, may hold values from 1.5 to 6
- w_qkv: bfloat16 [3072, 6144], P('slab', 'fsdp'), may hold values from -0.07252963 to 0.07252963
- w_out: bfloat16 [3072, 2048], P('slab', 'fsdp'), may hold values from -0.5 to 0.5
- rewards: float32 [12], replicated, may hold values from -4 to 4
Outputs:
- sample: bfloat16 [6144, 3072], P('slab', 'fsdp')
- grad_qkv: float32 [3072, 6144], P('slab', 'fsdp')
- grad_out: float32 [3072, 2048], P('slab', 'fsdp')
All inputs are finite; a program needn't handle non-finite values.
Results may differ from a plain program's by a relative error of at most 0.025.
The roundings to bfloat16 on the way count: a program that leaves them out, or rounds other values in their place, can miss the bound.
Values may be sent and summed in bfloat16 or wider, within the bound.
A program may use at most 64 MiB of HBM per device.

v0:
```python
import math

import jax
import jax.numpy as jnp
from jax import lax
from jax.sharding import PartitionSpec as P

TILE = 384
GH = 1


epsilon = 1e-06
noise_level = 0.5


def from_behind(array, axis, by):
    count = lax.axis_size(axis)
    pairs = [(i, i + by) for i in range(count) if 0 <= i + by < count]
    return lax.ppermute(array, axis, pairs)


def with_halo(cells, sides, width):
    for axis, dim in sides:
        count = lax.axis_size(axis)
        ends = count - 1
        head = lax.slice_in_dim(cells, 0, width, axis=dim)
        tail = lax.slice_in_dim(cells, cells.shape[dim] - width, cells.shape[dim], axis=dim)
        cells = jnp.concatenate(
            [
                lax.ppermute(tail, axis, [(i, (i + 1) % count) for i in range(ends)]),
                cells,
                lax.ppermute(head, axis, [((i + 1) % count, i) for i in range(ends)]),
            ],
            axis=dim,
        )
    return cells


def rms_rows(values, gain):
    return values * lax.rsqrt(jnp.mean(values * values, axis=-1, keepdims=True) + epsilon) * gain


def tile_allowed(tok_rows, tile_size, height_tiles):
    tile_number = jnp.arange(tok_rows) // tile_size
    time_tile = tile_number // height_tiles
    height_tile = tile_number % height_tiles
    near_time = jnp.abs(time_tile[:, None] - time_tile[None, :]) <= 1
    near_height = jnp.abs(height_tile[:, None] - height_tile[None, :]) <= 1
    return near_time & near_height


def contract_last(left, right):
    return lax.dot_general(
        left, right, (((1,), (1,)), ((), ())), preferred_element_type=jnp.float32
    )


def contract_first(left, right):
    return lax.dot_general(
        left, right, (((0,), (0,)), ((), ())), preferred_element_type=jnp.float32
    )


def norm_back(raw_values, gain, cotangent):
    return jax.vjp(lambda inner_values: rms_rows(inner_values, gain), raw_values)[1](cotangent)[0]


def neighbour_part(part, offset):
    return from_behind(part.astype(jnp.bfloat16), "slab", offset).astype(part.dtype)


def rounded_terms(terms):
    return lax.optimization_barrier(terms.astype(jnp.bfloat16)).astype(jnp.float32)


def shards(hidden, noise, norm_gain, qk_gain, w_qkv, w_out, rewards):
    tok_rows, model_width = hidden.shape
    head_size = qk_gain.shape[1]
    head_scale = 1.0 / math.sqrt(head_size)
    slab_count = lax.axis_size("slab")
    slab_index = lax.axis_index("slab")
    qkv_full, out_full = (
        lax.all_gather(w_qkv, "slab", axis=0, tiled=True),
        lax.all_gather(w_out, "slab", axis=0, tiled=True),
    )
    normed = rms_rows(hidden.astype(jnp.float32), norm_gain).astype(jnp.bfloat16)
    projected = jnp.dot(normed, qkv_full, preferred_element_type=jnp.float32)
    query_raw = projected[:, :head_size]
    key_raw = projected[:, head_size : 2 * head_size]
    value_raw = projected[:, 2 * head_size :]
    queries = rms_rows(query_raw, qk_gain[0]).astype(jnp.bfloat16)
    keys_own = rms_rows(key_raw, qk_gain[1]).astype(jnp.bfloat16)
    values = value_raw.astype(jnp.bfloat16)
    own_pair = jnp.concatenate([keys_own, values], axis=1)[None]
    pairs = with_halo(own_pair, (("slab", 0),), 1)
    keys_all = pairs[:, :, :head_size].reshape(3 * tok_rows, head_size)
    values_all = pairs[:, :, head_size:].reshape(3 * tok_rows, head_size)
    present = jnp.stack([slab_index > 0, slab_index >= 0, slab_index < slab_count - 1])
    allowed = (
        jnp.tile(tile_allowed(tok_rows, TILE, GH), (1, 3)) & jnp.repeat(present, tok_rows)[None, :]
    )
    scores = jnp.where(allowed, contract_last(queries, keys_all) * head_scale, -1e30)
    row_max = jnp.max(scores, axis=-1, keepdims=True)
    exponent_terms = jnp.exp(scores - row_max)
    row_total = jnp.sum(exponent_terms, axis=-1, keepdims=True)
    weights = exponent_terms / row_total
    weights_b = weights.astype(jnp.bfloat16)
    attended = jnp.dot(weights_b, values_all, preferred_element_type=jnp.float32).astype(
        jnp.bfloat16
    )
    partial_sum = contract_last(attended, out_full)
    branch_part = lax.psum_scatter(
        rounded_terms(partial_sum).astype(jnp.bfloat16), "fsdp", scatter_dimension=1, tiled=True
    )
    sample = (branch_part.astype(jnp.float32) + noise_level * noise.astype(jnp.float32)).astype(
        jnp.bfloat16
    )
    advantage = rewards[0] - jnp.mean(rewards)
    grad_factor = -advantage / noise_level
    grad_piece = (
        lax.all_gather(noise, "fsdp", axis=1, tiled=True).astype(jnp.float32) * grad_factor
    ).astype(jnp.bfloat16)
    attended_sum = jnp.dot(grad_piece, out_full, preferred_element_type=jnp.float32)
    grad_rows = contract_first(grad_piece, attended)
    attended_sum, grad_out_part = (attended_sum, grad_rows)
    attended_grad = attended_sum.astype(jnp.bfloat16)
    weight_grad = contract_last(attended_grad, values_all)
    row_delta = jnp.sum(weights * weight_grad, axis=-1, keepdims=True)
    dscore = (weights * (weight_grad - row_delta)).astype(jnp.bfloat16)
    dquery = jnp.dot(dscore, keys_all, preferred_element_type=jnp.float32) * head_scale
    key_grads_all = contract_first(dscore, queries) * head_scale
    value_grads_all = contract_first(weights_b, attended_grad)
    pair_grads = jnp.concatenate([key_grads_all, value_grads_all], axis=1).reshape(
        3, tok_rows, 2 * head_size
    )
    pair_grad = pair_grads[1] + neighbour_part(pair_grads[0], -1) + neighbour_part(pair_grads[2], 1)
    key_grad = pair_grad[:, :head_size]
    value_grad = pair_grad[:, head_size:]
    query_raw_grad = norm_back(query_raw, qk_gain[0], dquery)
    key_raw_grad = norm_back(key_raw, qk_gain[1], key_grad)
    qkv_grad = jnp.concatenate([query_raw_grad, key_raw_grad, value_grad], axis=1).astype(
        jnp.bfloat16
    )
    grad_qkv_part = contract_first(normed, qkv_grad)
    grad_qkv, grad_out = (
        lax.psum_scatter(
            grad_qkv_part.astype(jnp.bfloat16), "slab", scatter_dimension=0, tiled=True
        ).astype(jnp.float32),
        lax.psum_scatter(
            grad_out_part.astype(jnp.bfloat16), "slab", scatter_dimension=0, tiled=True
        ).astype(jnp.float32),
    )
    return (sample, grad_qkv, grad_out)


def solution(mesh):
    return jax.shard_map(
        shards,
        mesh=mesh,
        in_specs=(
            P("slab", None),
            P("slab", "fsdp"),
            P(),
            P(),
            P("slab", "fsdp"),
            P("slab", "fsdp"),
            P(),
        ),
        out_specs=(P("slab", "fsdp"), P("slab", "fsdp"), P("slab", "fsdp")),
        check_vma=False,
    )
```

profile of v0, /device:TPU:2, one launch (start us, length us, event | category | flops | bytes accessed | tf_op | source)
XLA Modules:
  0.0 386.5 jit_solution(3554068660045620314)
XLA Ops:
  7.2 0.7 all-gather.3.cloned.1.call-update
  8.0 0.7 all-gather.5.cloned.1.call-update
  9.8 1.3 reduce_sum.77
  12.4 0.8 slice_bitcast_fusion.1
  13.1 2.2 fusion
  15.4 47.2 %all_gather.10 = bf16[3072,128]{1,0:T(8,128)(2,1)S(1)} all-gather(bf16[192,128]{1,0:T(8,128)(2,1)S(1)} %copy-done.5), channel_id=1, replica_groups=mesh['slab'=16,'fsdp'=16] {'slab'}, dimensions={0}, use_global_device_ids=true | all-gather | bytes 835584 | tf_op jit(solution)/shard_map/all_gather | solution.py:84
  62.5 23.0 %all-gather.3.cloned.1.call-done = bf16[3072,384]{1,0:T(8,128)(2,1)} async-done(((bf16[192,384]{1,0:T(8,128)(2,1)}), bf16[3072,384]{1,0:T(8,128)(2,1)}) %all-gather.3.cloned.1.call-update) | async-done | bytes 2359312 | tf_op jit(solution)/shard_map/all_gather | solution.py:83
  85.5 3.9 %fusion.10 = f32[384,384]{0,1:T(8,128)S(1)} fusion(bf16[3072,384]{1,0:T(8,128)(2,1)} %all-gather.3.cloned.1.call-done, bf16[384,3072]{1,0:T(8,128)(2,1)} %param.7, f32[3072]{0:T(1024)S(1)} %copy-done.15, f32[384]{0:T(512)S(1)} %add_rsqrt_fusion), kind=kOutput, calls=%fused_computation.25 | convolution fusion | flops 910688256 | bytes 5322240 | tf_op jit(solution)/shard_map/dot_general | solution.py:87
  89.6 3.6 collective-permute-start
  93.2 1.3 collective-permute-start.1
  94.5 46.6 %all-gather.5.cloned.1.call-done = bf16[384,3072]{0,1:T(8,128)(2,1)} async-done(((bf16[384,192]{0,1:T(8,128)(2,1)}), bf16[384,3072]{0,1:T(8,128)(2,1)}) %all-gather.5.cloned.1.call-update) | async-done | bytes 2359312 | tf_op jit(solution)/shard_map/all_gather | solution.py:121
  141.1 2.5 fusion.8
  144.0 0.9 copy.19
  145.0 0.7 fusion.33
  146.1 2.3 multiply_reduce_fusion
  148.9 1.7 convolution_convert_fusion.2
  150.7 2.2 convolution_convert_fusion.1
  152.9 4.3 %copy.22 = bf16[384,3072]{0,1:T(8,128)(2,1)} copy(bf16[384,3072]{1,0:T(8,128)(2,1)} %convolution_convert_fusion.1) | data formatting | bytes 4718592
  157.8 1.7 multiply_convert_fusion.3
  160.5 1.3 collective-permute-start.2
  161.8 4.7 %collective-permute-start.3 = (bf16[384,256]{0,1:T(8,128)(2,1)S(1)}, bf16[384,256]{0,1:T(8,128)(2,1)S(1)}, u32[]{:S(2)}, u32[]{:S(2)}) collective-permute-start(bf16[384,256]{0,1:T(8,128)(2,1)S(1)} %get-tuple-element.21), channel_id=1, source_target_pairs={{0,16},{16,32},{32,48},{48,64},{64,80},{80,96},{96,112},{112,128},... | collective-permute-start | bytes 589832 | tf_op jit(solution)/shard_map/ppermute | solution.py:19
  166.6 3.5 collective-permute-done.2
  170.1 1.4 collective-permute-done.3
  172.3 3.2 convolution_convert_fusion
  175.5 0.9 copy-done.2
  176.6 44.3 %reduce-scatter.8.cloned.1.call-done = bf16[192,128]{1,0:T(8,128)(2,1)} async-done(((bf16[3072,128]{1,0:T(8,128)(2,1)}), bf16[192,128]{1,0:T(8,128)(2,1)}) %reduce-scatter.8.cloned.1.call-update) | async-done | bytes 49168 | tf_op jit(solution)/shard_map/reduce_scatter | solution.py:149
  220.8 1.4 convert_element_type.85
  222.3 79.2 %reduce-scatter.10.cloned.1.call-done = bf16[192,384]{1,0:T(8,128)(2,1)} async-done(((bf16[3072,384]{1,0:T(8,128)(2,1)}), bf16[192,384]{1,0:T(8,128)(2,1)}) %reduce-scatter.10.cloned.1.call-update) | async-done | bytes 147472
  301.5 1.0 copy.23
  302.6 0.8 copy.21
  303.4 74.9 %reduce-scatter.6.cloned.1.call-done = bf16[192,384]{1,0:T(8,128)(2,1)} async-done(((bf16[3072,384]{1,0:T(8,128)(2,1)}), bf16[192,384]{1,0:T(8,128)(2,1)}) %reduce-scatter.6.cloned.1.call-update) | async-done | bytes 147472 | tf_op jit(solution)/shard_map/reduce_scatter | solution.py:146
  378.3 1.6 convert_element_type.83
  (74 shorter events, 5.1 us)
Async XLA Ops:
  7.2 8.2 %copy-start.5 = (bf16[192,128]{1,0:T(8,128)(2,1)S(1)}, bf16[192,128]{1,0:T(8,128)(2,1)}, u32[]{:S(2)}) copy-start(bf16[192,128]{1,0:T(8,128)(2,1)} %param.12) | copy-start | bytes 147460
  7.2 78.3 %all-gather.3.cloned.1.call-start = ((), (), s32[]{:S(2)}) async-start(), calls=%async_computation.3 | async-start | bytes 2506752 | tf_op jit(solution)/shard_map/all_gather | solution.py:83
  7.9 133.2 %all-gather.5.cloned.1.call-start = ((), (), s32[]{:S(2)}) async-start(), calls=%async_computation.4 | async-start | bytes 2506752 | tf_op jit(solution)/shard_map/all_gather | solution.py:121
  8.7 212.2 %reduce-scatter.8.cloned.1.call-start = ((), (), s32[]{:S(2)}) async-start(), calls=%async_computation.6 | async-start | bytes 835584 | tf_op jit(solution)/shard_map/reduce_scatter | solution.py:149
  9.1 76.4 %copy-start.15 = (f32[3072]{0:T(1024)S(1)}, f32[3072]{0:T(1024)}, u32[]{:S(2)}) copy-start(f32[3072]{0:T(1024)} %param.9) | copy-start | bytes 36868
  13.1 76.3 %copy-start.6 = (f32[128]{0:T(128)}, f32[128]{0:T(128)S(1)}, u32[]{:S(2)}) copy-start(f32[128]{0:T(128)S(1)} %get-tuple-element.25) | copy-start | bytes 1540
  13.1 131.8 %copy-start.8 = (f32[128]{0:T(128)}, f32[128]{0:T(128)S(1)}, u32[]{:S(2)}) copy-start(f32[128]{0:T(128)S(1)} %get-tuple-element.24) | copy-start | bytes 1540
  15.4 74.0 %copy-start.11 = (f32[384]{0:T(512)}, f32[384]{0:T(512)S(1)}, u32[]{:S(2)}) copy-start(f32[384]{0:T(512)S(1)} %add_rsqrt_fusion) | copy-start | bytes 4612
  89.6 54.1 %collective-permute-start = (bf16[1,384,256]{1,2,0:T(8,128)(2,1)S(1)}, bf16[1,384,256]{1,2,0:T(8,128)(2,1)S(1)}, u32[]{:S(2)}, u32[]{:S(2)}) collective-permute-start(bf16[1,384,256]{1,2,0:T(8,128)(2,1)S(1)} %maximum_bitcast_fusion), channel_id=1, source_target_pairs={{0,16},{16,32},{32,48},{48,64},{64,80},{80,96},{96,112},{112,128},... | collective-permute-start | bytes 589832 | tf_op jit(solution)/shard_map/ppermute | solution.py:30
  93.2 50.5 %collective-permute-start.1 = (bf16[1,384,256]{1,2,0:T(8,128)(2,1)S(1)}, bf16[1,384,256]{1,2,0:T(8,128)(2,1)S(1)}, u32[]{:S(2)}, u32[]{:S(2)}) collective-permute-start(bf16[1,384,256]{1,2,0:T(8,128)(2,1)S(1)} %maximum_bitcast_fusion), channel_id=1, source_target_pairs={{16,0},{32,16},{48,32},{64,48},{80,64},{96,80},{112,96},{128,112},... | collective-permute-start | bytes 589832 | tf_op jit(solution)/shard_map/ppermute | solution.py:32
  143.6 2.5 copy-start.3
  144.9 1.2 copy-start.1
  146.1 2.8 copy-start.14
  150.6 150.9 %reduce-scatter.10.cloned.1.call-start = ((), (), s32[]{:S(2)}) async-start(), calls=%async_computation.7 | async-start | bytes 2506752
  157.1 0.7 copy-start.10
  157.2 2.4 copy-start.9
  157.2 221.1 %reduce-scatter.6.cloned.1.call-start = ((), (), s32[]{:S(2)}) async-start(), calls=%async_computation.5 | async-start | bytes 2506752 | tf_op jit(solution)/shard_map/reduce_scatter | solution.py:146
  157.8 2.1 copy-start.4
  160.0 6.6 %copy-start.13 = (f32[2,128]{1,0:T(2,128)S(1)}, f32[2,128]{1,0:T(2,128)}, u32[]{:S(2)}) copy-start(f32[2,128]{1,0:T(2,128)} %param.10) | copy-start | bytes 3076
  160.4 11.3 %copy-start.7 = (f32[128]{0:T(128)S(1)}, f32[128]{0:T(128)}, u32[]{:S(2)}) copy-start(f32[128]{0:T(128)} %copy-done.6) | copy-start | bytes 1540
  160.5 9.6 %collective-permute-start.2 = (bf16[384,256]{0,1:T(8,128)(2,1)S(1)}, bf16[384,256]{0,1:T(8,128)(2,1)S(1)}, u32[]{:S(2)}, u32[]{:S(2)}) collective-permute-start(bf16[384,256]{0,1:T(8,128)(2,1)S(1)} %get-tuple-element.20), channel_id=1, source_target_pairs={{16,0},{32,16},{48,32},{64,48},{80,64},{96,80},{112,96},{128,112},... | collective-permute-start | bytes 589832 | tf_op jit(solution)/shard_map/ppermute | solution.py:19
  161.8 9.8 %collective-permute-start.3 = (bf16[384,256]{0,1:T(8,128)(2,1)S(1)}, bf16[384,256]{0,1:T(8,128)(2,1)S(1)}, u32[]{:S(2)}, u32[]{:S(2)}) collective-permute-start(bf16[384,256]{0,1:T(8,128)(2,1)S(1)} %get-tuple-element.21), channel_id=1, source_target_pairs={{0,16},{16,32},{32,48},{48,64},{64,80},{80,96},{96,112},{112,128},... | collective-permute-start | bytes 589832 | tf_op jit(solution)/shard_map/ppermute | solution.py:19
  166.6 5.7 %copy-start = (bf16[384,3072]{1,0:T(8,128)(2,1)S(1)}, bf16[384,3072]{1,0:T(8,128)(2,1)}, u32[]{:S(2)}) copy-start(bf16[384,3072]{1,0:T(8,128)(2,1)} %param.7) | copy-start | bytes 7077892
  166.6 5.7 %copy-start.12 = (f32[384]{0:T(512)S(1)}, f32[384]{0:T(512)}, u32[]{:S(2)}) copy-start(f32[384]{0:T(512)} %copy-done.11) | copy-start | bytes 4612
  166.6 5.7 %copy-start.16 = (f32[3072]{0:T(1024)S(1)}, f32[3072]{0:T(1024)}, u32[]{:S(2)}) copy-start(f32[3072]{0:T(1024)} %param.9) | copy-start | bytes 36868
  175.5 0.9 copy-start.2
Sparse Core Ops, SparseCore 0:
  9.8 75.6 all-gather.2
  88.2 52.9 all-gather.4
  150.7 70.0 reduce-scatter.7
  225.6 75.9 reduce-scatter.9
  304.1 74.1 reduce-scatter.5
where the time goes:
time: 387 us; the launch traced here: 386 us
  waiting for transfers between devices  274 us (71%)
  blocking collectives  47.2 us (12%)
  matrix products  18.2 us (5%)
  between operations  15.5 us (4%)
  starting transfers between devices  11.1 us (3%)
  local copies, waits for them, and re-layouts  10.5 us (3%)
  other arithmetic  9.61 us (2%)
    unnamed x6, waiting for transfers between devices  80.6 us
    reduce_scatter x1, waiting for transfers between devices, shards(): lax.psum_scatter(grad_qkv_part.astype(jnp.bfloat16), 'slab', scatter_dime...  74.9 us
    all_gather x1, blocking collectives, shards(): lax.all_gather(w_out, 'slab', axis=0, tiled=True)  47.2 us
    all_gather x1, waiting for transfers between devices, shards(): lax.all_gather(noise, 'fsdp', axis=1, tiled=True).astype(jnp.float32)  46.6 us
    reduce_scatter x1, waiting for transfers between devices, shards(): lax.psum_scatter(grad_out_part.astype(jnp.bfloat16), 'slab', scatter_dime...  44.3 us
    all_gather x1, waiting for transfers between devices, shards(): lax.all_gather(w_qkv, 'slab', axis=0, tiled=True)  23 us
    unnamed x38, local copies, waits for them, and re-layouts  7.79 us
  transfers between devices with their start and end apart: 9, of which 7 were waited for; matrix products, arithmetic and copies ran while one was open for 7% of the time, Pallas kernels for 0%

commit v1 on v0

v1 whole, which is shorter than its diff:
```python
import math

import jax
import jax.numpy as jnp
from jax import lax
from jax.experimental import pallas as pl
from jax.experimental.pallas import tpu as pltpu
from jax.sharding import PartitionSpec as P

epsilon = 1e-06
noise_level = 0.5
MESH = pl.DeviceIdType.MESH
F32 = jnp.float32
BF16 = jnp.bfloat16
TOK = 384
HD = 128
ROWS = 192
HALF = 96
NZ = 8
NSEM = 128


def dot(left, right):
    return lax.dot_general(left, right, (((1,), (0,)), ((), ())), preferred_element_type=F32)


def dot_t(left, right):
    return lax.dot_general(left, right, (((1,), (1,)), ((), ())), preferred_element_type=F32)


def dot_first(left, right):
    return lax.dot_general(left, right, (((0,), (0,)), ((), ())), preferred_element_type=F32)


def kernel(
    hidden_ref, noise_ref, gain_ref, qk_gain_ref, wq_in, wo_in, rewards_ref,
    sample_ref, gq_ref, go_ref,
    wq, wo, bg, nrm_t, npair, row_scale, acc, att_t, q_t, dout_t,
    kv, grad_in, grad_out_buf, exps, wgs, w_b, ds_b,
    ht_send, ht_own, ht_sib, part, part_in, y_send, y_in,
    op_send, op_in, g_own, g_pair, ring_send, ring_in,
    ssem, rsem,
):
    s = lax.axis_index("slab")
    f = lax.axis_index("fsdp")
    y = s // NZ
    z = s % NZ
    core = f % 2
    yh = (f // 2) % 2
    x = f // 4

    def slab(flip, k):
        side = 1 - y if flip else y
        return side * NZ + (z + k + NZ) % NZ

    up = (slab(0, 1), f)
    down = (slab(0, -1), f)
    across = (slab(1, 0), f)
    sibling = (s, f + 1 - 2 * core)
    y_far = (s, f + 2 - 4 * yh)

    def x_dev(d):
        return (s, (f + 4 * d) % 16)

    has_left = s > 0
    has_right = s < 2 * NZ - 1
    left = ((s + 15) % 16, f)
    right = ((s + 1) % 16, f)

    sent = []
    names = {}

    def num(name):
        if name not in names:
            names[name] = len(names)
            assert len(names) <= NSEM
        return names[name]

    def copy_of(name, src, dst, to):
        i = num(name)
        return pltpu.make_async_remote_copy(
            src_ref=src, dst_ref=dst, send_sem=ssem.at[i], recv_sem=rsem.at[i],
            device_id=to, device_id_type=MESH,
        )

    def send(name, src, dst, to):
        copy = copy_of(name, src, dst, to)
        copy.start()
        sent.append(copy)

    def arrived(name, dst):
        copy_of(name, dst, dst, up).wait_recv()

    barrier = pltpu.get_barrier_semaphore()
    partners = [up, down, across, sibling, y_far, x_dev(1), x_dev(2), x_dev(3), left, right]
    for to in partners:
        pl.semaphore_signal(barrier, inc=1, device_id=to, device_id_type=MESH)

    rewards = rewards_ref[...]
    advantage = rewards[:, 0:1] - jnp.sum(rewards, axis=1, keepdims=True) * (1.0 / rewards.shape[1])
    factor = -advantage / noise_level
    noise_t = noise_ref[...].T
    bg[f] = (noise_t.astype(F32) * factor).astype(BF16)
    wq[s] = wq_in[...]
    wo[s] = wo_in[...]

    pl.semaphore_wait(barrier, len(partners))

    def gather_steps(tag, buf):
        def own():
            send(tag + "u0", buf.at[s], buf.at[s], up)
            send(tag + "d0", buf.at[s], buf.at[s], down)
            send(tag + "a0", buf.at[s], buf.at[s], across)

        def one(k, to, kind, flip=0, onto=None):
            block = buf.at[slab(flip, k)]
            if onto is not None:
                block = block.at[onto]
            send(kind, block, block, to)

        def first():
            arrived(tag + "u0", buf.at[slab(0, -1)])
            one(-1, up, tag + "u1")
            one(-1, across, tag + "a-")
            arrived(tag + "d0", buf.at[slab(0, 1)])
            one(1, down, tag + "d1")
            one(1, across, tag + "a+")

        def second():
            arrived(tag + "u1", buf.at[slab(0, -2)])
            one(-2, up, tag + "u2")
            arrived(tag + "d1", buf.at[slab(0, 2)])
            one(2, down, tag + "d2")

        def third():
            arrived(tag + "u2", buf.at[slab(0, -3)])
            one(-3, up, tag + "u3", onto=pl.ds(0, HALF))
            arrived(tag + "d2", buf.at[slab(0, 3)])
            one(3, down, tag + "d3", onto=pl.ds(HALF, HALF))

        def fourth():
            arrived(tag + "a0", buf.at[slab(1, 0)])
            arrived(tag + "a-", buf.at[slab(1, -1)])
            one(-1, up, tag + "u4", flip=1)
            arrived(tag + "a+", buf.at[slab(1, 1)])
            one(1, down, tag + "d4", flip=1)

        def fifth():
            arrived(tag + "u4", buf.at[slab(1, -2)])
            one(-2, up, tag + "u5", flip=1)
            arrived(tag + "d4", buf.at[slab(1, 2)])
            one(2, down, tag + "d5", flip=1)

        def sixth():
            arrived(tag + "u5", buf.at[slab(1, -3)])
            one(-3, up, tag + "u6", flip=1, onto=pl.ds(0, HALF))
            arrived(tag + "d5", buf.at[slab(1, 3)])
            one(3, down, tag + "d6", flip=1, onto=pl.ds(HALF, HALF))

        def last_own():
            arrived(tag + "u3", buf.at[slab(0, 4)].at[pl.ds(0, HALF)])
            arrived(tag + "d3", buf.at[slab(0, 4)].at[pl.ds(HALF, HALF)])

        def last():
            arrived(tag + "u6", buf.at[slab(1, 4)].at[pl.ds(0, HALF)])
            arrived(tag + "d6", buf.at[slab(1, 4)].at[pl.ds(HALF, HALF)])

        return own, first, second, third, fourth, fifth, sixth, last_own, last

    q_own, q_1, q_2, q_3, q_4, q_5, q_6, q_last_own, q_last = gather_steps("q", wq)
    o_own, o_1, o_2, o_3, o_4, o_5, o_6, o_last_own, o_last = gather_steps("o", wo)

    def project(*blocks):
        for flip, k in blocks:
            j = slab(flip, k)
            acc[...] += dot_first(wq[j], nrm_t[j])

    q_own()

    f_y = f + 2 - 4 * yh

    def block_x(base, d):
        return (base + 4 * d + 16) % 16

    send("ny", bg.at[f], bg.at[f], y_far)
    send("nx+", bg.at[f], bg.at[f], x_dev(1))
    send("nx-", bg.at[f], bg.at[f], x_dev(3))
    send("nc", bg.at[f], bg.at[f], sibling)

    def scales(i, carry):
        rows = pl.ds(pl.multiple_of(i * 48, 16), 48)
        values = hidden_ref[rows, :].astype(F32)
        mean = jnp.sum(values * values, axis=1, keepdims=True) * (1.0 / values.shape[1])
        row_scale[rows, :] = jnp.broadcast_to(lax.rsqrt(mean + epsilon), (48, 128))
        return carry

    lax.fori_loop(0, 8, scales, 0)
    q_1()

    def normalise(p, carry):
        cols = pl.ds(pl.multiple_of(p * 384, 128), 384)
        values = hidden_ref[:, cols].astype(F32) * row_scale[:, 0:1] * gain_ref[:, cols]
        turned = values.astype(BF16).T
        nrm_t[2 * p] = turned[:ROWS]
        nrm_t[2 * p + 1] = turned[ROWS:]
        return carry

    lax.fori_loop(0, 4, normalise, 0)
    q_2()
    lax.fori_loop(4, 8, normalise, 0)

    acc[...] = jnp.zeros_like(acc)
    other = (1 - y) * NZ + 4 * core
    q_3()
    send("np", nrm_t.at[pl.ds(other, 4)], npair.at[pl.ds(4 * core, 4)], across)
    o_own()
    arrived("ny", bg.at[f_y])
    send("yx+", bg.at[f_y], bg.at[f_y], x_dev(1))
    send("yx-", bg.at[f_y], bg.at[f_y], x_dev(3))
    send("yc", bg.at[f_y], bg.at[f_y], sibling)
    project((0, 0), (0, -1), (0, 1))
    q_4()
    o_1()
    project((0, -2), (0, 2))
    arrived("nx+", bg.at[block_x(f, -1)])
    send("nx2", bg.at[block_x(f, -1)], bg.at[block_x(f, -1)], x_dev(1))
    send("nc1", bg.at[block_x(f, -1)], bg.at[block_x(f, -1)], sibling)
    arrived("nx-", bg.at[block_x(f, 1)])
    send("nc3", bg.at[block_x(f, 1)], bg.at[block_x(f, 1)], sibling)
    q_5()
    o_2()
    project((0, -3), (0, 3), (1, 0))
    q_6()
    o_3()
    project((1, -1), (1, 1))
    arrived("yx-", bg.at[block_x(f_y, 1)])
    send("yx2", bg.at[block_x(f_y, 1)], bg.at[block_x(f_y, 1)], x_dev(3))
    send("yc3", bg.at[block_x(f_y, 1)], bg.at[block_x(f_y, 1)], sibling)
    arrived("yx+", bg.at[block_x(f_y, -1)])
    send("yc1", bg.at[block_x(f_y, -1)], bg.at[block_x(f_y, -1)], sibling)
    q_last_own()
    project((0, 4), (1, -2), (1, 2))
    arrived("nx2", bg.at[block_x(f, 2)])
    send("nc2", bg.at[block_x(f, 2)], bg.at[block_x(f, 2)], sibling)
    arrived("yx2", bg.at[block_x(f_y, 2)])
    send("yc2", bg.at[block_x(f_y, 2)], bg.at[block_x(f_y, 2)], sibling)
    o_4()
    project((1, -3), (1, 3))
    q_last()
    project((1, 4))

    def gain_of(i):
        turned = jnp.broadcast_to(qk_gain_ref[i : i + 1, :], (HD, HD)).T
        return jnp.concatenate([turned, turned, turned], axis=1)

    def scale_of(raw):
        return lax.rsqrt(jnp.sum(raw * raw, axis=0, keepdims=True) * (1.0 / HD) + epsilon)

    key_raw = acc[HD : 2 * HD, :]
    kv[1, 0] = (key_raw * scale_of(key_raw) * gain_of(1)).astype(BF16)
    kv[1, 1] = acc[2 * HD :, :].astype(BF16)

    @pl.when(has_right)
    def _():
        copy_of("kv>", kv.at[1], kv.at[0], right).start()

    @pl.when(has_left)
    def _():
        copy_of("kv<", kv.at[1], kv.at[2], left).start()

    query_raw = acc[0:HD, :]
    q_t[...] = (query_raw * scale_of(query_raw) * gain_of(0)).astype(BF16)

    @pl.when(jnp.logical_not(has_left))
    def _():
        kv[0] = jnp.zeros((2, HD, TOK), BF16)
        grad_in[0] = jnp.zeros((2, HD, TOK), BF16)

    @pl.when(jnp.logical_not(has_right))
    def _():
        kv[2] = jnp.zeros((2, HD, TOK), BF16)
        grad_in[1] = jnp.zeros((2, HD, TOK), BF16)

    arrived("np", npair.at[pl.ds(4 * core, 4)])
    send("npc", npair.at[pl.ds(4 * core, 4)], npair.at[pl.ds(4 * core, 4)], sibling)
    o_5()

    head_scale = 1.0 / math.sqrt(HD)

    def scores(col):
        value = dot(kv[col, 0].T, q_t[...]) * head_scale
        if col == 0:
            value = jnp.where(has_left, value, -1e30)
        if col == 2:
            value = jnp.where(has_right, value, -1e30)
        exps[col] = value
        return jnp.max(value, axis=0, keepdims=True)

    peak = scores(1)
    o_6()
    o_last_own()

    f_core = f + 1 - 2 * core
    f_ycore = f_y + 1 - 2 * core
    arrived("nc", bg.at[f_core])
    arrived("nc1", bg.at[block_x(f_core, -1)])
    arrived("nc2", bg.at[block_x(f_core, 2)])
    arrived("nc3", bg.at[block_x(f_core, 1)])
    arrived("yc", bg.at[f_ycore])
    arrived("yc1", bg.at[block_x(f_ycore, -1)])
    arrived("yc2", bg.at[block_x(f_ycore, 2)])
    arrived("yc3", bg.at[block_x(f_ycore, 1)])
    o_last()

    def out_grad(j, total):
        return total + dot_first(wo[j], bg[j])

    dout_t[...] = lax.fori_loop(0, 16, out_grad, jnp.zeros((HD, TOK), F32)).astype(BF16)

    @pl.when(has_left)
    def _():
        arrived("kv>", kv.at[0])

    peak = jnp.maximum(peak, scores(0))

    @pl.when(has_right)
    def _():
        arrived("kv<", kv.at[2])

    peak = jnp.maximum(peak, scores(2))
    total = jnp.zeros((1, TOK), F32)
    for col in range(3):
        value = jnp.exp(exps[col] - peak)
        exps[col] = value
        total = total + jnp.sum(value, axis=0, keepdims=True)
    attended = jnp.zeros((HD, TOK), F32)
    for col in range(3):
        value = exps[col] / total
        exps[col] = value
        w_b[col] = value.astype(BF16)
        attended = attended + dot(kv[col, 1], w_b[col])
    att_t[...] = attended.astype(BF16)

    def term_away(i, carry):
        ht_send[i] = dot(wo[2 * i + 1 - core], att_t[...]).astype(BF16)
        return carry

    lax.fori_loop(0, 8, term_away, 0)
    send("ht", ht_send, ht_sib, sibling)

    def out_part(i, carry):
        op_send[i] = dot_t(bg[(1 - y) * NZ + i], att_t[...]).astype(BF16)
        return carry

    lax.fori_loop(0, 8, out_part, 0)
    send("op", op_send, op_in, across)

    for col, name, to, ok in ((0, "dv<", left, has_left), (2, "dv>", right, has_right)):
        grad_out_buf[col // 2, 1] = dot_t(dout_t[...], w_b[col]).astype(BF16)
        landing = grad_in.at[1 - col // 2, 1]

        @pl.when(ok)
        def _(name=name, to=to, landing=landing, col=col):
            copy_of(name, grad_out_buf.at[col // 2, 1], landing, to).start()

    def term_own(i, carry):
        ht_own[i] = dot(wo[2 * i + core], att_t[...]).astype(BF16)
        return carry

    lax.fori_loop(0, 8, term_own, 0)

    delta = jnp.zeros((1, TOK), F32)
    for col in range(3):
        value = dot(kv[col, 1].T, dout_t[...])
        wgs[col] = value
        delta = delta + jnp.sum(exps[col] * value, axis=0, keepdims=True)
    for col in range(3):
        ds_b[col] = (exps[col] * (wgs[col] - delta)).astype(BF16)
    for col, name, to, ok in ((0, "dk<", left, has_left), (2, "dk>", right, has_right)):
        grad_out_buf[col // 2, 0] = (dot_t(q_t[...], ds_b[col]) * head_scale).astype(BF16)
        landing = grad_in.at[1 - col // 2, 0]

        @pl.when(ok)
        def _(name=name, to=to, landing=landing, col=col):
            copy_of(name, grad_out_buf.at[col // 2, 0], landing, to).start()

    def norm_back(raw, gain, cotangent):
        scale = scale_of(raw)
        inner = gain * cotangent
        mixed = jnp.sum(raw * inner, axis=0, keepdims=True) * (1.0 / HD)
        return scale * inner - raw * (scale * scale * scale * mixed)

    dq = (
        dot(kv[0, 0], ds_b[0]) + dot(kv[1, 0], ds_b[1]) + dot(kv[2, 0], ds_b[2])
    ) * head_scale
    g_own[0] = norm_back(acc[0:HD, :], gain_of(0), dq).astype(BF16)
    send("gq", g_own.at[0], g_pair.at[0], across)

    arrived("ht", ht_sib)

    def both(i, carry):
        part[i] = (ht_own[i].astype(F32) + ht_sib[i].astype(F32)).astype(BF16)
        return carry

    lax.fori_loop(0, 8, both, 0)
    for d in (1, 2, 3):
        send(
            "bx%d" % d,
            part.at[pl.ds(2 * ((x + d) % 4), 2)],
            part_in.at[d - 1],
            x_dev(d),
        )

    arrived("npc", npair.at[pl.ds(4 - 4 * core, 4)])
    arrived("op", op_in)

    def term(g, zd):
        j = y * NZ + zd
        if g == 3:
            return dot_t(bg[j], att_t[...]) + op_in[zd].astype(F32)
        return dot_t(nrm_t[j], g_own[g]) + dot_t(npair[zd], g_pair[g])

    first_half, second_half = pl.ds(0, HALF), pl.ds(HALF, HALF)

    def stage(g, st):
        if st == 4:
            value = term(g, (z + 4) % NZ).astype(BF16)
            for d, rows in ((0, first_half), (1, second_half)):
                ring_send[g, d, 3, rows, :] = value[rows.start : rows.start + HALF]
                send(
                    "r%d%d4" % (g, d),
                    ring_send.at[g, d, 3, rows],
                    ring_in.at[g, d, 3, rows],
                    (up, down)[d],
                )
            return
        for d in (0, 1):
            zd = (z + st) % NZ if d == 0 else (z - st + NZ) % NZ
            value = term(g, zd)
            if st == 3:
                rows = (first_half, second_half)[d]
                rest = (second_half, first_half)[d]
                arrived("r%d%d4" % (g, d), ring_in.at[g, d, 3, rows])
                ring_send[g, d, 2, rows, :] = (
                    value[rows.start : rows.start + HALF] + ring_in[g, d, 3, rows, :].astype(F32)
                ).astype(BF16)
                ring_send[g, d, 2, rest, :] = value[rest.start : rest.start + HALF].astype(BF16)
            else:
                arrived("r%d%d%d" % (g, d, st + 1), ring_in.at[g, d, st])
                ring_send[g, d, st - 1] = (value + ring_in[g, d, st].astype(F32)).astype(BF16)
            send(
                "r%d%d%d" % (g, d, st),
                ring_send.at[g, d, st - 1],
                ring_in.at[g, d, st - 1],
                (up, down)[d],
            )

    def finish(g):
        value = term(g, z)
        for d in (0, 1):
            arrived("r%d%d1" % (g, d), ring_in.at[g, d, 0])
            value = value + ring_in[g, d, 0].astype(F32)
        if g == 3:
            go_ref[...] = value
        else:
            gq_ref[:, g * HD : (g + 1) * HD] = value

    stage(3, 4)

    dv = dot_t(dout_t[...], w_b[1])

    @pl.when(has_right)
    def _():
        arrived("dv<", grad_in.at[1, 1])

    @pl.when(has_left)
    def _():
        arrived("dv>", grad_in.at[0, 1])

    g_own[2] = (dv + grad_in[1, 1].astype(F32) + grad_in[0, 1].astype(F32)).astype(BF16)
    send("gv", g_own.at[2], g_pair.at[2], across)

    arrived("gq", g_pair.at[0])
    stage(0, 4)
    stage(3, 3)

    dk = dot_t(q_t[...], ds_b[1]) * head_scale

    @pl.when(has_right)
    def _():
        arrived("dk<", grad_in.at[1, 0])

    @pl.when(has_left)
    def _():
        arrived("dk>", grad_in.at[0, 0])

    dk = dk + grad_in[1, 0].astype(F32) + grad_in[0, 0].astype(F32)
    g_own[1] = norm_back(acc[HD : 2 * HD, :], gain_of(1), dk).astype(BF16)
    send("gk", g_own.at[1], g_pair.at[1], across)
    arrived("gv", g_pair.at[2])
    stage(2, 4)
    stage(0, 3)
    stage(3, 2)
    arrived("gk", g_pair.at[1])
    stage(1, 4)
    stage(2, 3)
    stage(0, 2)
    stage(3, 1)

    for d in (1, 2, 3):
        arrived("bx%d" % d, part_in.at[d - 1])

    def x_sum(h):
        value = part[2 * x + h].astype(F32)
        for d in range(3):
            value = value + part_in[d, h].astype(F32)
        return value

    y_send[...] = x_sum(1 - yh).astype(BF16)
    send("by", y_send, y_in, y_far)

    stage(1, 3)
    stage(2, 2)
    stage(0, 1)
    finish(3)
    stage(1, 2)
    stage(2, 1)
    finish(0)
    stage(1, 1)
    finish(2)
    arrived("by", y_in)
    branch = (x_sum(yh) + y_in[...].astype(F32)).astype(BF16)
    out_t = (branch.astype(F32) + noise_level * noise_ref[...].T.astype(F32)).astype(BF16)
    sample_ref[...] = out_t.T
    finish(1)

    for copy in sent:
        copy.wait_send()

    @pl.when(has_right)
    def _():
        copy_of("kv>", kv.at[1], kv.at[0], right).wait_send()
        copy_of("dv>", grad_out_buf.at[1, 1], grad_in.at[0, 1], right).wait_send()
        copy_of("dk>", grad_out_buf.at[1, 0], grad_in.at[0, 0], right).wait_send()

    @pl.when(has_left)
    def _():
        copy_of("kv<", kv.at[1], kv.at[2], left).wait_send()
        copy_of("dv<", grad_out_buf.at[0, 1], grad_in.at[1, 1], left).wait_send()
        copy_of("dk<", grad_out_buf.at[0, 0], grad_in.at[1, 0], left).wait_send()


def shards(hidden, noise, norm_gain, qk_gain, w_qkv, w_out, rewards):
    vmem = pl.BlockSpec(memory_space=pltpu.VMEM)
    block = (ROWS, TOK)
    head = (HD, TOK)
    scratch = [
        pltpu.VMEM((16, ROWS, 3 * HD), BF16),
        pltpu.VMEM((16, ROWS, HD), BF16),
        pltpu.VMEM((16, *block), BF16),
        pltpu.VMEM((16, *block), BF16),
        pltpu.VMEM((8, *block), BF16),
        pltpu.VMEM((TOK, 128), F32),
        pltpu.VMEM((3 * HD, TOK), F32),
        pltpu.VMEM(head, BF16),
        pltpu.VMEM(head, BF16),
        pltpu.VMEM(head, BF16),
        pltpu.VMEM((3, 2, *head), BF16),
        pltpu.VMEM((2, 2, *head), BF16),
        pltpu.VMEM((2, 2, *head), BF16),
        pltpu.VMEM((3, TOK, TOK), F32),
        pltpu.VMEM((3, TOK, TOK), F32),
        pltpu.VMEM((3, TOK, TOK), BF16),
        pltpu.VMEM((3, TOK, TOK), BF16),
        pltpu.VMEM((8, *block), BF16),
        pltpu.VMEM((8, *block), BF16),
        pltpu.VMEM((8, *block), BF16),
        pltpu.VMEM((8, *block), BF16),
        pltpu.VMEM((3, 2, *block), BF16),
        pltpu.VMEM(block, BF16),
        pltpu.VMEM(block, BF16),
        pltpu.VMEM((8, ROWS, HD), BF16),
        pltpu.VMEM((8, ROWS, HD), BF16),
        pltpu.VMEM((3, *head), BF16),
        pltpu.VMEM((3, *head), BF16),
        pltpu.VMEM((4, 2, 4, ROWS, HD), BF16),
        pltpu.VMEM((4, 2, 4, ROWS, HD), BF16),
        pltpu.SemaphoreType.DMA((NSEM,)),
        pltpu.SemaphoreType.DMA((NSEM,)),
    ]
    return pl.pallas_call(
        kernel,
        out_shape=(
            jax.ShapeDtypeStruct((TOK, ROWS), BF16),
            jax.ShapeDtypeStruct((ROWS, 3 * HD), F32),
            jax.ShapeDtypeStruct((ROWS, HD), F32),
        ),
        in_specs=[vmem] * 7,
        out_specs=(vmem, vmem, vmem),
        scratch_shapes=scratch,
        compiler_params=pltpu.CompilerParams(
            collective_id=0, has_side_effects=True, vmem_limit_bytes=56 * 1024 * 1024
        ),
    )(
        hidden,
        noise,
        norm_gain.reshape(1, -1),
        qk_gain,
        w_qkv,
        w_out,
        rewards.reshape(1, -1),
    )


def solution(mesh):
    return jax.shard_map(
        shards,
        mesh=mesh,
        in_specs=(
            P("slab", None),
            P("slab", "fsdp"),
            P(),
            P(),
            P("slab", "fsdp"),
            P("slab", "fsdp"),
            P(),
        ),
        out_specs=(P("slab", "fsdp"), P("slab", "fsdp"), P("slab", "fsdp")),
        check_vma=False,
    )
```

time: 387 us -> 104 us (0.27)
  waiting for transfers between devices: 274 us -> 0 us
  Pallas kernels: 0 us -> 96.4 us
  blocking collectives: 47.2 us -> 0 us
  matrix products: 18.2 us -> 0 us
  between operations: 15.5 us -> 0.64 us
  starting transfers between devices: 11.1 us -> 0 us
  other arithmetic: 9.61 us -> 0 us
    reduce_scatter x2 -> x0, waiting for transfers between devices: 119 us -> none  [the longest x1 74.9 us: shards(): lax.psum_scatter(grad_qkv_part.astype(jnp.bfloat16), 'slab', scatter_dime...]
    pallas_call x0 -> x1, Pallas kernels: none -> 96.4 us  [shards(): pl.pallas_call(kernel, out_shape=(jax.ShapeDtypeStruct((TOK, ROWS), BF16)...]
    unnamed x6 -> x0, waiting for transfers between devices: 80.6 us -> none
    all_gather x2 -> x0, waiting for transfers between devices: 69.6 us -> none  [the longest x1 46.6 us: shards(): lax.all_gather(noise, 'fsdp', axis=1, tiled=True).astype(jnp.float32)]
    all_gather x1 -> x0, blocking collectives: 47.2 us -> none  [shards(): lax.all_gather(w_out, 'slab', axis=0, tiled=True)]
    dot_general x11 -> x0, matrix products: 18.2 us -> none  [the longest x4 5.72 us: contract_first(): lax.dot_general(left, right, (((0,), (0,)), ((), ())), preferred_element_...]
    ppermute x4 -> x0, starting transfers between devices: 10.9 us -> none  [the longest x2 6.03 us: from_behind(): return lax.ppermute(array, axis, pairs)]
    ppermute x4 -> x0, waiting for transfers between devices: 4.97 us -> none  [the longest x2 4.97 us: from_behind(): return lax.ppermute(array, axis, pairs)]
  transfers between devices with their start and end apart: 9 -> 0, of which waited for: 7 -> 0; matrix products, arithmetic and copies ran while one was open for 7% -> 0% of each run, Pallas kernels for 0% -> 0%
where the time goes in v1:
time: 104 us
  Pallas kernels  96.4 us (93%)
  local copies, waits for them, and re-layouts  6.67 us (6%)
    pallas_call x1, Pallas kernels, shards(): pl.pallas_call(kernel, out_shape=(jax.ShapeDtypeStruct((TOK, ROWS), BF16)...  96.4 us
    unnamed x3, local copies, waits for them, and re-layouts  4.96 us

profile of v1, /device:TPU:2, one launch (start us, length us, event | category | flops | bytes accessed | tf_op | source)
XLA Modules:
  0.0 103.7 jit_solution(4660209881073335831)
XLA Ops:
  0.6 1.7 %copy.10.noise_ref = bf16[384,192]{1,0:T(8,128)(2,1)} copy(bf16[384,192]{0,1:T(8,128)(2,1)} %param.8) | data formatting | bytes 294912 | tf_op args[1]
  2.4 96.4 %shard_map.94 = (bf16[384,192]{1,0:T(8,128)(2,1)}, f32[192,384]{1,0:T(8,128)}, f32[192,128]{1,0:T(8,128)}) custom-call(bf16[384,3072]{1,0:T(8,128)(2,1)} %hidden_ref.1, bf16[384,192]{1,0:T(8,128)(2,1)} %copy.10.noise_ref, f32[1,3072]{1,0:T(1,128)} %bitcast.2, f32[2,128]{1,0:T(2,128)} %qk_gain_ref.1, bf16[192,384]{1,0:T(8,128)(2,1)} %wq_in.1, ...), custom_call_target="tpu_custom_call" | custom-call | tf_op jit(solution)/shard_map/pallas_call | solution.py:591
  98.8 1.7 %copy.11 = bf16[384,192]{0,1:T(8,128)(2,1)} copy(bf16[384,192]{1,0:T(8,128)(2,1)} %get-tuple-element.3) | data formatting | bytes 294912 | tf_op jit(solution)/shard_map/pallas_call | solution.py:591
  100.5 1.7 %copy.14 = f32[192,384]{1,0:T(8,128)} copy(f32[192,384]{1,0:T(8,128)} %get-tuple-element.10) | data formatting | bytes 589824
  102.2 1.5 %copy.15 = f32[192,128]{1,0:T(8,128)} copy(f32[192,128]{1,0:T(8,128)} %get-tuple-element.11) | data formatting | bytes 196608

commit v2 on v1

v2 whole, which is shorter than its diff:
```python
import math

import jax
import jax.numpy as jnp
from jax import lax
from jax.experimental import pallas as pl
from jax.experimental.pallas import tpu as pltpu
from jax.sharding import PartitionSpec as P

epsilon = 1e-06
noise_level = 0.5
MESH = pl.DeviceIdType.MESH
F32 = jnp.float32
BF16 = jnp.bfloat16
TOK = 384
HD = 128
ROWS = 192
HALF = 96
NZ = 8
NSEM = 192


def dot(left, right):
    return lax.dot_general(left, right, (((1,), (0,)), ((), ())), preferred_element_type=F32)


def dot_t(left, right):
    return lax.dot_general(left, right, (((1,), (1,)), ((), ())), preferred_element_type=F32)


def dot_first(left, right):
    return lax.dot_general(left, right, (((0,), (0,)), ((), ())), preferred_element_type=F32)


def kernel(
    hidden_hbm, noise_ref, gain_ref, qk_gain_ref, wq_in, wo_in, rewards_ref,
    sample_ref, gq_ref, go_ref,
    hidden_ref, wq, wo, bg, nrm_t, npair, row_scale, acc, dacc, att_t, q_t, dout_t,
    kv, grad_in, grad_out_buf, exps, wgs, w_b, ds_b,
    ht_send, ht_own, ht_sib, part, part_in, y_send, y_in,
    op_send, op_in, g_own, g_pair, ctr, ring_send, ring_in,
    ssem, rsem, hsem,
):
    s = lax.axis_index("slab")
    f = lax.axis_index("fsdp")
    y = s // NZ
    z = s % NZ
    core = f % 2
    yh = (f // 2) % 2
    x = f // 4

    def slab(flip, k):
        side = 1 - y if flip else y
        return side * NZ + (z + k + NZ) % NZ

    up = (slab(0, 1), f)
    down = (slab(0, -1), f)
    across = (slab(1, 0), f)
    sibling = (s, f + 1 - 2 * core)
    y_far = (s, f + 2 - 4 * yh)

    def x_dev(d):
        return (s, (f + 4 * d) % 16)

    has_left = s > 0
    has_right = s < 2 * NZ - 1
    left = ((s + 15) % 16, f)
    right = ((s + 1) % 16, f)

    sent = []
    names = {}

    def num(name):
        if name not in names:
            names[name] = len(names)
            assert len(names) <= NSEM
        return names[name]

    def copy_of(name, src, dst, to):
        i = num(name)
        return pltpu.make_async_remote_copy(
            src_ref=src, dst_ref=dst, send_sem=ssem.at[i], recv_sem=rsem.at[i],
            device_id=to, device_id_type=MESH,
        )

    def send(name, src, dst, to):
        copy = copy_of(name, src, dst, to)
        copy.start()
        sent.append(copy)

    def arrived(name, dst):
        copy_of(name, dst, dst, up).wait_recv()

    barrier = pltpu.get_barrier_semaphore()
    partners = [up, down, across, sibling, y_far, x_dev(1), x_dev(2), x_dev(3), left, right]
    for to in partners:
        pl.semaphore_signal(barrier, inc=1, device_id=to, device_id_type=MESH)
    hidden_copy = pltpu.make_async_copy(hidden_hbm, hidden_ref, hsem)
    hidden_copy.start()

    rewards = rewards_ref[...]
    advantage = rewards[:, 0:1] - jnp.sum(rewards, axis=1, keepdims=True) * (1.0 / rewards.shape[1])
    factor = -advantage / noise_level
    bg[f] = (noise_ref[...].astype(F32) * factor).astype(BF16)
    wq[s] = wq_in[...]
    wo[s] = wo_in[...]

    pl.semaphore_wait(barrier, len(partners))

    def rows_of(h):
        return pl.ds(HALF * h, HALF)

    def q_piece(flip, k, h):
        return wq.at[slab(flip, k)].at[rows_of(h)]

    incoming = [(0, 1, 0), (0, 1, 1), (0, 2, 0), (0, 2, 1), (0, 3, 0), (0, 3, 1), (0, 4, 0),
                (1, 2, 0), (1, 2, 1), (1, 3, 0), (1, 3, 1), (1, 4, 0)]
    onward = {0: 2, 1: 3, 2: 4, 3: 5, 4: 6, 7: 9, 8: 10, 9: 11}

    def q_start():
        for i in (0, 1):
            send("qu%d" % i, q_piece(0, 0, i), q_piece(0, 0, i), up)
            send("qd%d" % i, q_piece(0, 0, 1 - i), q_piece(0, 0, 1 - i), down)
            send("qa%d" % i, q_piece(0, 0, i), q_piece(0, 0, i), across)

    def q_event(n):
        flip, k, second = incoming[n]
        for link, sign, h, to in (("qu", -1, second, up), ("qd", 1, 1 - second, down)):
            block = q_piece(flip, sign * k, h)
            arrived("%s%d" % (link, n), block)
            if n in onward:
                send("%s%d" % (link, onward[n]), block, block, to)
            if n in (0, 1):
                send("qa%d" % (2 + 2 * n + (sign + 1) // 2), block, block, across)

    def q_across(n):
        for link, sign, h, to in (("qu", -1, n, up), ("qd", 1, 1 - n, down)):
            block = q_piece(1, sign, h)
            arrived("qa%d" % (2 + 2 * n + (sign + 1) // 2), block)
            send("%s%d" % (link, 7 + n), block, block, to)

    def q_across_own():
        arrived("qa0", q_piece(1, 0, 0))
        arrived("qa1", q_piece(1, 0, 1))

    def o_start():
        block = wo.at[s]
        send("ou0", block, block, up)
        send("od0", block, block, down)
        send("oa0", block, block, across)

    def o_event(n):
        for i, (link, sign, h, to) in enumerate((("ou", -1, 0, up), ("od", 1, 1, down))):
            block = wo.at[slab(0, sign * (n + 1))]
            if n == 3:
                block = block.at[rows_of(h)]
            arrived("%s%d" % (link, n), block)
            if n < 2:
                send("%s%d" % (link, n + 1), block, block, to)
            if n == 2:
                send("%s3" % link, block.at[rows_of(h)], block.at[rows_of(h)], to)
            send("oa%d" % (1 + 2 * n + i), block, block, across)

    def o_across(n):
        if n == 0:
            arrived("oa0", wo.at[slab(1, 0)])
            return
        for i, (sign, h) in enumerate(((-1, 0), (1, 1))):
            block = wo.at[slab(1, sign * n)]
            if n == 4:
                block = block.at[rows_of(h)]
            arrived("oa%d" % (2 * n - 1 + i), block)

    def project(*blocks):
        for flip, k in blocks:
            j = slab(flip, k)
            acc[...] += dot_first(wq[j], nrm_t[j])

    q_start()

    f_y = f + 2 - 4 * yh

    def block_x(base, d):
        return (base + 4 * d + 16) % 16

    def pass_bg(name, j, to):
        send(name, bg.at[j], bg.at[j], to)

    pass_bg("nx+", f, x_dev(1))
    pass_bg("nx-", f, x_dev(3))
    pass_bg("nc", f, sibling)
    hidden_copy.wait()

    def scales(i, carry):
        rows = pl.ds(pl.multiple_of(i * 48, 16), 48)
        values = hidden_ref[rows, :].astype(F32)
        mean = jnp.sum(values * values, axis=1, keepdims=True) * (1.0 / values.shape[1])
        row_scale[rows, :] = jnp.broadcast_to(lax.rsqrt(mean + epsilon), (48, 128))
        return carry

    lax.fori_loop(0, 8, scales, 0)

    def normalise(p, carry):
        cols = pl.ds(pl.multiple_of(p * 384, 128), 384)
        values = hidden_ref[:, cols].astype(F32) * row_scale[:, 0:1] * gain_ref[:, cols]
        turned = values.astype(BF16).T
        nrm_t[2 * p] = turned[:ROWS]
        nrm_t[2 * p + 1] = turned[ROWS:]
        return carry

    lax.fori_loop(0, 4, normalise, 0)
    q_event(0)
    lax.fori_loop(4, 8, normalise, 0)
    acc[...] = jnp.zeros_like(acc)
    dacc[...] = jnp.zeros_like(dacc)
    q_event(1)
    pass_bg("ny", f, y_far)
    project((0, 0))
    q_event(2)
    arrived("nx+", bg.at[block_x(f, -1)])
    pass_bg("nx2", block_x(f, -1), x_dev(1))
    pass_bg("nc1", block_x(f, -1), sibling)
    arrived("nx-", bg.at[block_x(f, 1)])
    pass_bg("nc3", block_x(f, 1), sibling)
    project((0, -1), (0, 1))
    q_event(3)
    q_event(4)
    q_across(0)
    m = 2 * x + core
    m_core = 2 * x + 1 - core
    send("np", nrm_t.at[(1 - y) * NZ + m], npair.at[m], across)
    project((0, -2), (0, 2))
    q_event(5)
    q_across(1)
    q_across_own()
    project((0, -3), (0, 3), (1, 0))
    arrived("ny", bg.at[f_y])
    pass_bg("yx+", f_y, x_dev(1))
    pass_bg("yx-", f_y, x_dev(3))
    pass_bg("yc", f_y, sibling)
    q_event(6)
    project((0, 4), (1, -1), (1, 1))
    q_event(7)
    q_event(8)
    project((1, -2), (1, 2))
    arrived("yx-", bg.at[block_x(f_y, 1)])
    pass_bg("yx2", block_x(f_y, 1), x_dev(3))
    pass_bg("yc3", block_x(f_y, 1), sibling)
    arrived("yx+", bg.at[block_x(f_y, -1)])
    pass_bg("yc1", block_x(f_y, -1), sibling)
    arrived("nx2", bg.at[block_x(f, 2)])
    pass_bg("nc2", block_x(f, 2), sibling)
    q_event(9)
    o_start()
    arrived("np", npair.at[m])
    for d in (1, 2, 3):
        send("np%d" % d, npair.at[m], npair.at[m], x_dev(d))
    send("npc0", npair.at[m], npair.at[m], sibling)
    q_event(10)
    project((1, -3), (1, 3))
    q_event(11)
    project((1, 4))

    def gain_of(i):
        turned = jnp.broadcast_to(qk_gain_ref[i : i + 1, :], (HD, HD)).T
        return jnp.concatenate([turned, turned, turned], axis=1)

    def scale_of(raw):
        return lax.rsqrt(jnp.sum(raw * raw, axis=0, keepdims=True) * (1.0 / HD) + epsilon)

    key_raw = acc[HD : 2 * HD, :]
    kv[1, 0] = (key_raw * scale_of(key_raw) * gain_of(1)).astype(BF16)
    kv[1, 1] = acc[2 * HD :, :].astype(BF16)

    @pl.when(has_right)
    def _():
        copy_of("k>", kv.at[1, 0], kv.at[0, 0], right).start()
        copy_of("v>", kv.at[1, 1], kv.at[0, 1], right).start()

    @pl.when(has_left)
    def _():
        copy_of("k<", kv.at[1, 0], kv.at[2, 0], left).start()
        copy_of("v<", kv.at[1, 1], kv.at[2, 1], left).start()

    query_raw = acc[0:HD, :]
    q_t[...] = (query_raw * scale_of(query_raw) * gain_of(0)).astype(BF16)

    @pl.when(jnp.logical_not(has_left))
    def _():
        kv[0] = jnp.zeros((2, HD, TOK), BF16)
        grad_in[0] = jnp.zeros((2, HD, TOK), BF16)

    @pl.when(jnp.logical_not(has_right))
    def _():
        kv[2] = jnp.zeros((2, HD, TOK), BF16)
        grad_in[1] = jnp.zeros((2, HD, TOK), BF16)

    o_event(0)
    head_scale = 1.0 / math.sqrt(HD)

    def scores(col):
        value = dot(kv[col, 0].T, q_t[...]) * head_scale
        if col == 0:
            value = jnp.where(has_left, value, -1e30)
        if col == 2:
            value = jnp.where(has_right, value, -1e30)
        exps[col] = value
        return jnp.max(value, axis=0, keepdims=True)

    def weight_grad(col):
        wgs[col] = dot(kv[col, 1].T, dout_t[...])

    peak = scores(1)

    arrived("yx2", bg.at[block_x(f_y, 2)])
    pass_bg("yc2", block_x(f_y, 2), sibling)
    for d in (1, 2, 3):
        chunk = npair.at[(m - 2 * d + 8) % 8]
        arrived("np%d" % d, chunk)
        send("npc%d" % d, chunk, chunk, sibling)
    f_core = f + 1 - 2 * core
    f_ycore = f_y + 1 - 2 * core
    arrived("nc", bg.at[f_core])
    arrived("nc1", bg.at[block_x(f_core, -1)])
    arrived("nc2", bg.at[block_x(f_core, 2)])
    arrived("nc3", bg.at[block_x(f_core, 1)])
    arrived("yc", bg.at[f_ycore])
    arrived("yc1", bg.at[block_x(f_ycore, -1)])
    arrived("yc3", bg.at[block_x(f_ycore, 1)])
    arrived("yc2", bg.at[block_x(f_ycore, 2)])

    def out_grad(*blocks):
        total = dacc[...]
        for flip, k in blocks:
            j = slab(flip, k)
            total = total + dot_first(wo[j], bg[j])
        dacc[...] = total

    o_event(1)
    out_grad((0, 0), (0, -1), (0, 1))
    o_event(2)
    out_grad((0, -2), (0, 2))
    @pl.when(has_left)
    def _():
        arrived("k>", kv.at[0, 0])

    @pl.when(has_right)
    def _():
        arrived("k<", kv.at[2, 0])

    o_event(3)
    peak = jnp.maximum(peak, scores(0))
    peak = jnp.maximum(peak, scores(2))
    o_across(0)
    o_across(1)
    out_grad((0, -3), (0, 3), (0, 4), (1, 0), (1, -1), (1, 1))
    total = jnp.zeros((1, TOK), F32)
    for col in range(3):
        value = jnp.exp(exps[col] - peak)
        exps[col] = value
        total = total + jnp.sum(value, axis=0, keepdims=True)
    for col in range(3):
        value = exps[col] / total
        exps[col] = value
        w_b[col] = value.astype(BF16)
    o_across(2)
    o_across(3)
    out_grad((1, -2), (1, 2), (1, -3), (1, 3))
    o_across(4)
    out_grad((1, 4))
    dout_t[...] = dacc[...].astype(BF16)
    weight_grad(1)
    @pl.when(has_left)
    def _():
        arrived("v>", kv.at[0, 1])

    @pl.when(has_right)
    def _():
        arrived("v<", kv.at[2, 1])

    weight_grad(0)
    weight_grad(2)
    delta = jnp.zeros((1, TOK), F32)
    for col in range(3):
        delta = delta + jnp.sum(exps[col] * wgs[col], axis=0, keepdims=True)
    for col in range(3):
        ds_b[col] = (exps[col] * (wgs[col] - delta)).astype(BF16)

    def halo_grad(kind, name, left_hand, right_hand, scale):
        for col, to, ok, mark in ((0, left, has_left, "<"), (2, right, has_right, ">")):
            value = dot_t(left_hand[...], right_hand[col])
            if scale is not None:
                value = value * scale
            grad_out_buf[col // 2, kind] = value.astype(BF16)

            @pl.when(ok)
            def _(col=col, to=to, mark=mark):
                copy_of(
                    name + mark, grad_out_buf.at[col // 2, kind], grad_in.at[1 - col // 2, kind], to
                ).start()

    def halo_wait(kind, name):
        @pl.when(has_right)
        def _():
            arrived(name + "<", grad_in.at[1, kind])

        @pl.when(has_left)
        def _():
            arrived(name + ">", grad_in.at[0, kind])

        return grad_in[1, kind].astype(F32) + grad_in[0, kind].astype(F32)

    halo_grad(0, "dk", q_t, ds_b, head_scale)

    def norm_back(raw, gain, cotangent):
        scale = scale_of(raw)
        inner = gain * cotangent
        mixed = jnp.sum(raw * inner, axis=0, keepdims=True) * (1.0 / HD)
        return scale * inner - raw * (scale * scale * scale * mixed)

    dq = (
        dot(kv[0, 0], ds_b[0]) + dot(kv[1, 0], ds_b[1]) + dot(kv[2, 0], ds_b[2])
    ) * head_scale
    g_own[0] = norm_back(acc[0:HD, :], gain_of(0), dq).astype(BF16)
    send("g0", g_own.at[0], g_pair.at[0], across)
    halo_grad(1, "dv", dout_t, w_b, None)

    attended = dot(kv[0, 1], w_b[0]) + dot(kv[1, 1], w_b[1]) + dot(kv[2, 1], w_b[2])
    att_t[...] = attended.astype(BF16)

    def terms(phase, own, buf):
        h = 1 - yh if phase == 0 else yh
        c = core if own else 1 - core
        for i in range(4):
            buf[phase, i] = dot(wo[4 * i + 2 * h + c], att_t[...]).astype(BF16)

    def terms_sum(phase):
        arrived("ht%d" % phase, ht_sib.at[phase])
        for i in range(4):
            part[phase, i] = (
                ht_own[phase, i].astype(F32) + ht_sib[phase, i].astype(F32)
            ).astype(BF16)
        for d in (2, 1, 3):
            send(
                "bx%d%d" % (phase, d),
                part.at[phase, (x + d) % 4],
                part_in.at[phase, d - 1],
                x_dev(d),
            )

    def x_sum(phase):
        value = part[phase, x].astype(F32)
        for d in (1, 2, 3):
            arrived("bx%d%d" % (phase, d), part_in.at[phase, d - 1])
            value = value + part_in[phase, d - 1].astype(F32)
        return value

    terms(0, False, ht_send)
    send("ht0", ht_send.at[0], ht_sib.at[0], sibling)
    terms(0, True, ht_own)
    terms(1, False, ht_send)
    send("ht1", ht_send.at[1], ht_sib.at[1], sibling)
    terms_sum(0)

    def own_rows(g):
        rows = pl.ds(y * NZ, NZ)
        if g == 3:
            value = dot_t(bg[rows].reshape(NZ * ROWS, TOK), att_t[...])
        else:
            value = dot_t(nrm_t[rows].reshape(NZ * ROWS, TOK), g_own[g])
        ctr[g] = value.reshape(NZ, ROWS, HD)

    def op_piece(k):
        i = (z + k + NZ) % NZ
        op_send[i] = dot_t(bg[(1 - y) * NZ + i], att_t[...]).astype(BF16)
        send("op%d" % (k + 3), op_send.at[i], op_in.at[i], across)

    op_piece(4)
    dk = dot_t(q_t[...], ds_b[1]) * head_scale
    dk = dk + halo_wait(0, "dk")
    g_own[1] = norm_back(acc[HD : 2 * HD, :], gain_of(1), dk).astype(BF16)
    send("g1", g_own.at[1], g_pair.at[1], across)
    dv = dot_t(dout_t[...], w_b[1])
    g_own[2] = (dv + halo_wait(1, "dv")).astype(BF16)
    send("g2", g_own.at[2], g_pair.at[2], across)
    terms(1, True, ht_own)
    terms_sum(1)
    own_rows(0)

    arrived("npc0", npair.at[m_core])
    for d in (1, 2, 3):
        arrived("npc%d" % d, npair.at[(m_core - 2 * d + 8) % 8])

    def term(g, k):
        zd = (z + k + NZ) % NZ
        if g == 3:
            arrived("op%d" % (k + 3), op_in.at[zd])
            return ctr[3, zd] + op_in[zd].astype(F32)
        return ctr[g, zd] + dot_t(npair[zd], g_pair[g])

    def stage(g, st):
        if st == 4:
            if g < 3:
                arrived("g%d" % g, g_pair.at[g])
            value = term(g, 4).astype(BF16)
            for d in (0, 1):
                rows = rows_of(d)
                ring_send[g, d, 3, rows, :] = value[HALF * d : HALF * (d + 1)]
                send(
                    "r%d%d4" % (g, d),
                    ring_send.at[g, d, 3, rows],
                    ring_in.at[g, d, 3, rows],
                    (up, down)[d],
                )
            return
        for d in (0, 1):
            value = term(g, st if d == 0 else -st)
            if st == 3:
                rows, rest = rows_of(d), rows_of(1 - d)
                arrived("r%d%d4" % (g, d), ring_in.at[g, d, 3, rows])
                ring_send[g, d, 2, rows, :] = (
                    value[HALF * d : HALF * (d + 1)] + ring_in[g, d, 3, rows, :].astype(F32)
                ).astype(BF16)
                ring_send[g, d, 2, rest, :] = value[HALF * (1 - d) : HALF * (2 - d)].astype(BF16)
            else:
                arrived("r%d%d%d" % (g, d, st + 1), ring_in.at[g, d, st])
                ring_send[g, d, st - 1] = (value + ring_in[g, d, st].astype(F32)).astype(BF16)
            send(
                "r%d%d%d" % (g, d, st),
                ring_send.at[g, d, st - 1],
                ring_in.at[g, d, st - 1],
                (up, down)[d],
            )

    def finish(g):
        value = term(g, 0)
        for d in (0, 1):
            arrived("r%d%d1" % (g, d), ring_in.at[g, d, 0])
            value = value + ring_in[g, d, 0].astype(F32)
        if g == 3:
            go_ref[...] = value
        else:
            gq_ref[:, g * HD : (g + 1) * HD] = value

    stage(0, 4)
    own_rows(1)
    own_rows(2)
    op_piece(3)
    op_piece(-3)
    own_rows(3)
    stage(1, 4)
    stage(0, 3)
    stage(2, 4)
    op_piece(2)
    op_piece(-2)
    stage(3, 4)
    stage(1, 3)
    stage(0, 2)
    op_piece(1)
    op_piece(-1)
    op_piece(0)
    y_send[...] = x_sum(0).astype(BF16)
    send("by", y_send, y_in, y_far)
    stage(2, 3)
    stage(3, 3)
    stage(1, 2)
    stage(0, 1)
    stage(2, 2)
    stage(3, 2)
    stage(1, 1)
    finish(0)
    stage(2, 1)
    stage(3, 1)
    finish(1)
    near = x_sum(1)
    arrived("by", y_in)
    branch = (near + y_in[...].astype(F32)).astype(BF16)
    sample_ref[...] = (branch.astype(F32) + noise_level * noise_ref[...].astype(F32)).astype(BF16)
    finish(2)
    finish(3)

    for copy in sent:
        copy.wait_send()

    @pl.when(has_right)
    def _():
        copy_of("k>", kv.at[1, 0], kv.at[0, 0], right).wait_send()
        copy_of("v>", kv.at[1, 1], kv.at[0, 1], right).wait_send()
        copy_of("dv>", grad_out_buf.at[1, 1], grad_in.at[0, 1], right).wait_send()
        copy_of("dk>", grad_out_buf.at[1, 0], grad_in.at[0, 0], right).wait_send()

    @pl.when(has_left)
    def _():
        copy_of("k<", kv.at[1, 0], kv.at[2, 0], left).wait_send()
        copy_of("v<", kv.at[1, 1], kv.at[2, 1], left).wait_send()
        copy_of("dv<", grad_out_buf.at[0, 1], grad_in.at[1, 1], left).wait_send()
        copy_of("dk<", grad_out_buf.at[0, 0], grad_in.at[1, 0], left).wait_send()


def hand_over(a_ref, b_ref, c_ref, a_out, b_out, c_out):
    a_out[...] = a_ref[...]
    b_out[...] = b_ref[...]
    c_out[...] = c_ref[...]


def shards(hidden, noise, norm_gain, qk_gain, w_qkv, w_out, rewards):
    vmem = pl.BlockSpec(memory_space=pltpu.VMEM)
    anywhere = pl.BlockSpec(memory_space=pl.ANY)
    block = (ROWS, TOK)
    head = (HD, TOK)
    scratch = [
        pltpu.VMEM(hidden.shape, BF16),
        pltpu.VMEM((16, ROWS, 3 * HD), BF16),
        pltpu.VMEM((16, ROWS, HD), BF16),
        pltpu.VMEM((16, *block), BF16),
        pltpu.VMEM((16, *block), BF16),
        pltpu.VMEM((8, *block), BF16),
        pltpu.VMEM((TOK, 128), F32),
        pltpu.VMEM((3 * HD, TOK), F32),
        pltpu.VMEM(head, F32),
        pltpu.VMEM(head, BF16),
        pltpu.VMEM(head, BF16),
        pltpu.VMEM(head, BF16),
        pltpu.VMEM((3, 2, *head), BF16),
        pltpu.VMEM((2, 2, *head), BF16),
        pltpu.VMEM((2, 2, *head), BF16),
        pltpu.VMEM((3, TOK, TOK), F32),
        pltpu.VMEM((3, TOK, TOK), F32),
        pltpu.VMEM((3, TOK, TOK), BF16),
        pltpu.VMEM((3, TOK, TOK), BF16),
        pltpu.VMEM((2, 4, *block), BF16),
        pltpu.VMEM((2, 4, *block), BF16),
        pltpu.VMEM((2, 4, *block), BF16),
        pltpu.VMEM((2, 4, *block), BF16),
        pltpu.VMEM((2, 3, *block), BF16),
        pltpu.VMEM(block, BF16),
        pltpu.VMEM(block, BF16),
        pltpu.VMEM((8, ROWS, HD), BF16),
        pltpu.VMEM((8, ROWS, HD), BF16),
        pltpu.VMEM((3, *head), BF16),
        pltpu.VMEM((3, *head), BF16),
        pltpu.VMEM((4, 8, ROWS, HD), F32),
        pltpu.VMEM((4, 2, 4, ROWS, HD), BF16),
        pltpu.VMEM((4, 2, 4, ROWS, HD), BF16),
        pltpu.SemaphoreType.DMA((NSEM,)),
        pltpu.SemaphoreType.DMA((NSEM,)),
        pltpu.SemaphoreType.DMA,
    ]
    outs = (
        jax.ShapeDtypeStruct((ROWS, TOK), BF16),
        jax.ShapeDtypeStruct((ROWS, 3 * HD), F32),
        jax.ShapeDtypeStruct((ROWS, HD), F32),
    )
    results = pl.pallas_call(
        kernel,
        out_shape=outs,
        in_specs=[anywhere] + [vmem] * 6,
        out_specs=(vmem, vmem, vmem),
        scratch_shapes=scratch,
        compiler_params=pltpu.CompilerParams(
            collective_id=0, has_side_effects=True, vmem_limit_bytes=56 * 1024 * 1024
        ),
    )(
        hidden,
        noise.T,
        norm_gain.reshape(1, -1),
        qk_gain,
        w_qkv,
        w_out,
        rewards.reshape(1, -1),
    )
    sample_t, grad_qkv, grad_out = pl.pallas_call(
        hand_over, out_shape=outs, in_specs=[vmem] * 3, out_specs=(vmem, vmem, vmem)
    )(*results)
    return sample_t.T, grad_qkv, grad_out


def solution(mesh):
    return jax.shard_map(
        shards,
        mesh=mesh,
        in_specs=(
            P("slab", None),
            P("slab", "fsdp"),
            P(),
            P(),
            P("slab", "fsdp"),
            P("slab", "fsdp"),
            P(),
        ),
        out_specs=(P("slab", "fsdp"), P("slab", "fsdp"), P("slab", "fsdp")),
        check_vma=False,
    )
```

time: 104 us -> 90.7 us (0.87)
  Pallas kernels: 96.4 us -> 89.6 us
  local copies, waits for them, and re-layouts: 6.67 us -> 0 us
    pallas_call x1 -> x2, Pallas kernels: 96.4 us -> 89.6 us  [the longest x1 87.8 us: shards(): pl.pallas_call(kernel, out_shape=outs, in_specs=[anywhere] + [vmem] * 6,...]
    unnamed x3 -> x0, local copies, waits for them, and re-layouts: 4.96 us -> none
    pallas_call x1 -> x0, local copies, waits for them, and re-layouts: 1.71 us -> none  [shards(): pl.pallas_call(kernel, out_shape=(jax.ShapeDtypeStruct((TOK, ROWS), BF16)...]
where the time goes in v2:
time: 90.7 us; the launch traced here: 90.3 us
  Pallas kernels  89.6 us (99%)
    pallas_call x1, Pallas kernels, shards(): pl.pallas_call(kernel, out_shape=outs, in_specs=[anywhere] + [vmem] * 6,...  87.8 us
    pallas_call x1, Pallas kernels, shards(): pl.pallas_call(hand_over, out_shape=outs, in_specs=[vmem] * 3, out_specs=...  1.86 us

profile of v2, /device:TPU:2, one launch (start us, length us, event | category | flops | bytes accessed | tf_op | source)
XLA Modules:
  0.0 90.3 jit_solution(3560029691868824472)
XLA Ops:
  0.6 87.8 %shard_map.94 = (bf16[192,384]{1,0:T(8,128)(2,1)}, f32[192,384]{1,0:T(8,128)}, f32[192,128]{1,0:T(8,128)}) custom-call(bf16[384,3072]{1,0:T(8,128)(2,1)} %hidden_hbm.1, bf16[192,384]{1,0:T(8,128)(2,1)} %bitcast.4, f32[1,3072]{1,0:T(1,128)} %bitcast.5, f32[2,128]{1,0:T(2,128)} %qk_gain_ref.1, bf16[192,384]{1,0:T(8,128)(2,1)} %wq_in.1, ...), custom_call_target="tpu_custom_call" | custom-call | tf_op jit(solution)/shard_map/pallas_call | solution.py:654
  88.4 1.9 %shard_map.95 = (bf16[192,384]{1,0:T(8,128)(2,1)}, f32[192,384]{1,0:T(8,128)}, f32[192,128]{1,0:T(8,128)}) custom-call(bf16[192,384]{1,0:T(8,128)(2,1)} %get-tuple-element.9.a_ref, f32[192,384]{1,0:T(8,128)} %get-tuple-element.10.b_ref, f32[192,128]{1,0:T(8,128)} %get-tuple-element.11.c_ref), custom_call_target="tpu_custom_call" | custom-call | tf_op jit(solution)/shard_map/pallas_call | solution.py:672

commit v3 on v2

v3 whole, which is shorter than its diff:
```python
import math

import jax
import jax.numpy as jnp
from jax import lax
from jax.experimental import pallas as pl
from jax.experimental.pallas import tpu as pltpu
from jax.sharding import PartitionSpec as P

epsilon = 1e-06
noise_level = 0.5
MESH = pl.DeviceIdType.MESH
F32 = jnp.float32
BF16 = jnp.bfloat16
TOK = 384
HD = 128
ROWS = 192
HALF = 96
NZ = 8
NSEM = 192


def dot(left, right):
    return lax.dot_general(left, right, (((1,), (0,)), ((), ())), preferred_element_type=F32)


def dot_t(left, right):
    return lax.dot_general(left, right, (((1,), (1,)), ((), ())), preferred_element_type=F32)


def dot_first(left, right):
    return lax.dot_general(left, right, (((0,), (0,)), ((), ())), preferred_element_type=F32)


def kernel(
    hidden_hbm, noise_hbm, gain_ref, qk_gain_ref, wq_hbm, wo_hbm, rewards_ref,
    sample_ref, gq_ref, go_ref,
    hidden_ref, noise_ref, wq, wo, bg, bpair, nrm_t, npair, row_scale, acc, dacc, q_t, dout_t,
    kv, q_in, dout_in, stats, stats_in, exps, wgs, w_b, ds_b,
    ht_send, ht_own, ht_sib, part, part_in, y_send, y_in,
    g_own, g_pair, ctr, ring_send, ring_in,
    ssem, rsem, hsem,
):
    s = lax.axis_index("slab")
    f = lax.axis_index("fsdp")
    y = s // NZ
    z = s % NZ
    core = f % 2
    yh = (f // 2) % 2
    x = f // 4

    def slab(flip, k):
        side = 1 - y if flip else y
        return side * NZ + (z + k + NZ) % NZ

    up = (slab(0, 1), f)
    down = (slab(0, -1), f)
    across = (slab(1, 0), f)
    sibling = (s, f + 1 - 2 * core)
    y_far = (s, f + 2 - 4 * yh)
    beyond = (slab(1, 0), f + 2 - 4 * yh)

    def x_dev(d):
        return (s, (f + 4 * d) % 16)

    has_left = s > 0
    has_right = s < 2 * NZ - 1
    left = ((s + 15) % 16, f)
    right = ((s + 1) % 16, f)

    sent = []
    names = {}

    def num(name):
        if name not in names:
            names[name] = len(names)
            assert len(names) <= NSEM
        return names[name]

    def copy_of(name, src, dst, to):
        i = num(name)
        return pltpu.make_async_remote_copy(
            src_ref=src, dst_ref=dst, send_sem=ssem.at[i], recv_sem=rsem.at[i],
            device_id=to, device_id_type=MESH,
        )

    def send(name, src, dst, to):
        copy = copy_of(name, src, dst, to)
        copy.start()
        sent.append(copy)

    def arrived(name, dst):
        copy_of(name, dst, dst, up).wait_recv()

    barrier = pltpu.get_barrier_semaphore()
    partners = [up, down, across, sibling, y_far, x_dev(1), x_dev(2), x_dev(3), left, right, beyond]
    for to in partners:
        pl.semaphore_signal(barrier, inc=1, device_id=to, device_id_type=MESH)
    noise_copy = pltpu.make_async_copy(noise_hbm, noise_ref, hsem.at[0])
    wq_copy = pltpu.make_async_copy(wq_hbm, wq.at[s], hsem.at[1])
    wo_copy = pltpu.make_async_copy(wo_hbm, wo.at[s], hsem.at[2])
    hidden_copy = pltpu.make_async_copy(hidden_hbm, hidden_ref, hsem.at[3])
    for copy in (noise_copy, wq_copy, wo_copy, hidden_copy):
        copy.start()

    rewards = rewards_ref[...]
    advantage = rewards[:, 0:1] - jnp.sum(rewards, axis=1, keepdims=True) * (1.0 / rewards.shape[1])
    factor = -advantage / noise_level
    noise_copy.wait()
    bg[f] = (noise_ref[...].astype(F32) * factor).astype(BF16)
    wq_copy.wait()
    wo_copy.wait()

    pl.semaphore_wait(barrier, len(partners))

    halo_sent = []

    def halo_send(name, src, landing):
        @pl.when(has_right)
        def _():
            copy_of(name + ">", src, landing(0), right).start()

        @pl.when(has_left)
        def _():
            copy_of(name + "<", src, landing(1), left).start()

        halo_sent.append((name, src, landing))

    def halo_wait(name, landing):
        @pl.when(has_left)
        def _():
            arrived(name + ">", landing(0))

        @pl.when(has_right)
        def _():
            arrived(name + "<", landing(1))

    def k_at(side):
        return kv.at[2 * side, 0]

    def v_at(side):
        return kv.at[2 * side, 1]

    def q_at(side):
        return q_in.at[side]

    def dout_at(side):
        return dout_in.at[side]

    def stats_at(side):
        return stats_in.at[side, pl.ds(0, 2)]

    def delta_at(side):
        return stats_in.at[side, 2]

    def rows_of(h):
        return pl.ds(HALF * h, HALF)

    def q_piece(flip, k, h):
        return wq.at[slab(flip, k)].at[rows_of(h)]

    incoming = [(0, 1, 0), (0, 1, 1), (0, 2, 0), (0, 2, 1), (0, 3, 0), (0, 3, 1), (0, 4, 0),
                (1, 2, 0), (1, 3, 0), (1, 3, 1), (1, 4, 0)]
    onward = {0: 2, 1: 3, 2: 4, 3: 5, 4: 6, 7: 8, 8: 10}

    def q_start():
        for i in (0, 1):
            send("qu%d" % i, q_piece(0, 0, i), q_piece(0, 0, i), up)
            send("qd%d" % i, q_piece(0, 0, 1 - i), q_piece(0, 0, 1 - i), down)

    def q_event(n):
        flip, k, second = incoming[n]
        for link, sign, h, to in (("qu", -1, second, up), ("qd", 1, 1 - second, down)):
            block = q_piece(flip, sign * k, h)
            arrived("%s%d" % (link, n), block)
            if n in onward:
                send("%s%d" % (link, onward[n]), block, block, to)
            if n in (0, 1, 3):
                send("%sa%d" % (link, n), block, block, across)

    def q_across(n, onto):
        k, second = incoming[n][1:]
        for link, sign, h, to in (("qu", -1, second, up), ("qd", 1, 1 - second, down)):
            block = q_piece(1, sign * k, h)
            arrived("%sa%d" % (link, n), block)
            if onto is not None:
                send("%s%d" % (link, onto), block, block, to)

    def q_across_own():
        arrived("qa0", q_piece(1, 0, 0))
        arrived("qa1", q_piece(1, 0, 1))

    def o_start():
        block = wo.at[s]
        send("ou0", block, block, up)
        send("od0", block, block, down)
        send("oa0", block, block, across)

    def o_event(n):
        for i, (link, sign, h, to) in enumerate((("ou", -1, 0, up), ("od", 1, 1, down))):
            block = wo.at[slab(0, sign * (n + 1))]
            if n == 3:
                block = block.at[rows_of(h)]
            arrived("%s%d" % (link, n), block)
            if n < 2:
                send("%s%d" % (link, n + 1), block, block, to)
            if n == 2:
                send("%s3" % link, block.at[rows_of(h)], block.at[rows_of(h)], to)
            send("oa%d" % (1 + 2 * n + i), block, block, across)

    def o_across(n):
        if n == 0:
            arrived("oa0", wo.at[slab(1, 0)])
            return
        for i, (sign, h) in enumerate(((-1, 0), (1, 1))):
            block = wo.at[slab(1, sign * n)]
            if n == 4:
                block = block.at[rows_of(h)]
            arrived("oa%d" % (2 * n - 1 + i), block)

    def project(*blocks):
        for flip, k in blocks:
            j = slab(flip, k)
            acc[...] += dot_first(wq[j], nrm_t[j])

    q_start()

    f_y = f + 2 - 4 * yh

    def block_x(base, d):
        return (base + 4 * d + 16) % 16

    def pass_bg(name, j, to):
        send(name, bg.at[j], bg.at[j], to)

    pass_bg("ny", f, y_far)
    pass_bg("nx+", f, x_dev(1))
    pass_bg("nx-", f, x_dev(3))
    pass_bg("nc", f, sibling)
    o_start()
    hidden_copy.wait()

    def scales(i, carry):
        rows = pl.ds(pl.multiple_of(i * 48, 16), 48)
        values = hidden_ref[rows, :].astype(F32)
        mean = jnp.sum(values * values, axis=1, keepdims=True) * (1.0 / values.shape[1])
        row_scale[rows, :] = jnp.broadcast_to(lax.rsqrt(mean + epsilon), (48, 128))
        return carry

    lax.fori_loop(0, 8, scales, 0)

    def normalise(p, carry):
        cols = pl.ds(pl.multiple_of(p * 384, 128), 384)
        values = hidden_ref[:, cols].astype(F32) * row_scale[:, 0:1] * gain_ref[:, cols]
        turned = values.astype(BF16).T
        nrm_t[2 * p] = turned[:ROWS]
        nrm_t[2 * p + 1] = turned[ROWS:]
        return carry

    lax.fori_loop(0, 4, normalise, 0)
    q_event(0)
    lax.fori_loop(4, 8, normalise, 0)
    acc[...] = jnp.zeros_like(acc)
    dacc[...] = jnp.zeros_like(dacc)
    q_event(1)
    m = 2 * x + core
    m_core = 2 * x + 1 - core
    send("np", nrm_t.at[(1 - y) * NZ + m], npair.at[m], beyond)
    o_event(0)
    project((0, 0))
    arrived("nx+", bg.at[block_x(f, -1)])
    pass_bg("nx2", block_x(f, -1), x_dev(1))
    pass_bg("nc1", block_x(f, -1), sibling)
    arrived("nx-", bg.at[block_x(f, 1)])
    pass_bg("nc3", block_x(f, 1), sibling)
    arrived("ny", bg.at[f_y])
    pass_bg("yx+", f_y, x_dev(1))
    pass_bg("yx-", f_y, x_dev(3))
    pass_bg("yc", f_y, sibling)
    def bp_index(y_of, yh_of, x_of, core_of):
        far = (x_of // 2 + y_of) % 2
        return (x_of + far) % 2 * 4 + (yh_of + far) % 2 * 2 + core_of

    b_out = bp_index(1 - y, 1 - yh, x, core)
    send("bp", bg.at[(1 - y) * NZ + b_out], bpair.at[b_out], beyond)
    q_event(2)
    project((0, -1), (0, 1))
    q_event(3)
    for i in (0, 1):
        send("qa%d" % i, q_piece(0, 0, i), q_piece(0, 0, i), across)
    o_event(1)
    q_event(4)
    q_across(0, 7)
    project((0, -2), (0, 2))
    q_event(5)
    arrived("yx-", bg.at[block_x(f_y, 1)])
    pass_bg("yx2", block_x(f_y, 1), x_dev(3))
    pass_bg("yc3", block_x(f_y, 1), sibling)
    arrived("yx+", bg.at[block_x(f_y, -1)])
    pass_bg("yc1", block_x(f_y, -1), sibling)
    arrived("nx2", bg.at[block_x(f, 2)])
    pass_bg("nc2", block_x(f, 2), sibling)
    o_event(2)
    q_across(1, None)
    project((0, -3), (0, 3))
    q_event(6)
    o_event(3)
    arrived("np", npair.at[m])
    for d in (1, 2, 3):
        send("np%d" % d, npair.at[m], npair.at[m], x_dev(d))
    send("npc0", npair.at[m], npair.at[m], sibling)
    project((0, 4), (1, -1), (1, 1))
    q_event(7)
    q_across(3, 9)
    project((1, -2), (1, 2))
    q_event(8)
    arrived("yx2", bg.at[block_x(f_y, 2)])
    pass_bg("yc2", block_x(f_y, 2), sibling)
    q_across_own()
    q_event(9)
    b_in = bp_index(y, yh, x, core)
    arrived("bp", bpair.at[b_in])
    for d in (1, 2, 3):
        send("bp%d" % d, bpair.at[b_in], bpair.at[b_in], x_dev(d))
    send("bpc0", bpair.at[b_in], bpair.at[b_in], sibling)
    project((1, -3), (1, 3), (1, 0))
    def out_grad(*blocks):
        total = dacc[...]
        for flip, k in blocks:
            j = slab(flip, k)
            total = total + dot_first(wo[j], bg[j])
        dacc[...] = total

    q_event(10)
    project((1, 4))
    def gain_of(i):
        turned = jnp.broadcast_to(qk_gain_ref[i : i + 1, :], (HD, HD)).T
        return jnp.concatenate([turned, turned, turned], axis=1)

    def scale_of(raw):
        return lax.rsqrt(jnp.sum(raw * raw, axis=0, keepdims=True) * (1.0 / HD) + epsilon)

    key_raw = acc[HD : 2 * HD, :]
    kv[1, 0] = (key_raw * scale_of(key_raw) * gain_of(1)).astype(BF16)
    halo_send("k", kv.at[1, 0], k_at)
    kv[1, 1] = acc[2 * HD :, :].astype(BF16)

    query_raw = acc[0:HD, :]
    q_t[...] = (query_raw * scale_of(query_raw) * gain_of(0)).astype(BF16)

    for side, ok in ((0, has_left), (1, has_right)):

        @pl.when(jnp.logical_not(ok))
        def _(side=side):
            kv[2 * side] = jnp.zeros((2, HD, TOK), BF16)
            q_in[side] = jnp.zeros((HD, TOK), BF16)
            dout_in[side] = jnp.zeros((HD, TOK), BF16)
            stats_in[side] = jnp.ones((3, 8, TOK), F32)

    head_scale = 1.0 / math.sqrt(HD)

    def scores(col):
        value = dot(kv[col, 0].T, q_t[...]) * head_scale
        if col == 0:
            value = jnp.where(has_left, value, -1e30)
        if col == 2:
            value = jnp.where(has_right, value, -1e30)
        exps[col] = value
        return jnp.max(value, axis=0, keepdims=True)

    def weight_grad(col):
        wgs[col] = dot(kv[col, 1].T, dout_t[...])

    peak = scores(1)

    halo_send("v", kv.at[1, 1], v_at)
    f_core = f + 1 - 2 * core
    f_ycore = f_y + 1 - 2 * core
    arrived("nc", bg.at[f_core])
    arrived("nc1", bg.at[block_x(f_core, -1)])
    arrived("nc2", bg.at[block_x(f_core, 2)])
    arrived("nc3", bg.at[block_x(f_core, 1)])
    arrived("yc", bg.at[f_ycore])
    arrived("yc1", bg.at[block_x(f_ycore, -1)])
    arrived("yc3", bg.at[block_x(f_ycore, 1)])
    arrived("yc2", bg.at[block_x(f_ycore, 2)])

    out_grad((0, 0), (0, -1), (0, 1), (0, -2), (0, 2))
    o_across(0)
    o_across(1)
    out_grad((0, -3), (0, 3), (1, 0), (1, -1), (1, 1))
    o_across(2)
    out_grad((0, 4), (1, -2), (1, 2))
    o_across(3)
    out_grad((1, -3), (1, 3))
    o_across(4)
    out_grad((1, 4))
    dout_t[...] = dacc[...].astype(BF16)
    halo_send("dout", dout_t, dout_at)
    halo_send("q", q_t, q_at)
    for d in (1, 2, 3):
        chunk = npair.at[(m - 2 * d + 8) % 8]
        arrived("np%d" % d, chunk)
        send("npc%d" % d, chunk, chunk, sibling)
    for d in (1, 2, 3):
        chunk = bpair.at[bp_index(y, yh, (x + 4 - d) % 4, core)]
        arrived("bp%d" % d, chunk)
        send("bpc%d" % d, chunk, chunk, sibling)
    weight_grad(1)
    halo_wait("k", k_at)
    peak = jnp.maximum(peak, scores(0))
    peak = jnp.maximum(peak, scores(2))
    total = jnp.zeros((1, TOK), F32)
    for col in range(3):
        value = jnp.exp(exps[col] - peak)
        exps[col] = value
        total = total + jnp.sum(value, axis=0, keepdims=True)
    stats[0] = jnp.broadcast_to(peak, (8, TOK))
    stats[1] = jnp.broadcast_to(total, (8, TOK))
    halo_send("stats", stats.at[pl.ds(0, 2)], stats_at)
    for col in range(3):
        value = exps[col] / total
        exps[col] = value
        w_b[col] = value.astype(BF16)
    halo_wait("v", v_at)
    attended = dot(kv[0, 1], w_b[0]) + dot(kv[1, 1], w_b[1]) + dot(kv[2, 1], w_b[2])
    g_own[3] = attended.astype(BF16)
    send("g3", g_own.at[3], g_pair.at[3], across)

    def terms(phase, own, buf):
        h = 1 - yh if phase == 0 else yh
        c = core if own else 1 - core
        for i in range(4):
            buf[phase, i] = dot(wo[4 * i + 2 * h + c], g_own[3]).astype(BF16)

    def terms_sum(phase):
        arrived("ht%d" % phase, ht_sib.at[phase])
        for i in range(4):
            part[phase, i] = (
                ht_own[phase, i].astype(F32) + ht_sib[phase, i].astype(F32)
            ).astype(BF16)
        for d in (2, 1, 3):
            send(
                "bx%d%d" % (phase, d),
                part.at[phase, (x + d) % 4],
                part_in.at[phase, d - 1],
                x_dev(d),
            )

    def x_sum(phase):
        value = part[phase, x].astype(F32)
        for d in (1, 2, 3):
            arrived("bx%d%d" % (phase, d), part_in.at[phase, d - 1])
            value = value + part_in[phase, d - 1].astype(F32)
        return value

    def own_rows(g):
        tokens = bg if g == 3 else nrm_t
        value = dot_t(tokens[pl.ds(y * NZ, NZ)].reshape(NZ * ROWS, TOK), g_own[g])
        ctr[g] = value.reshape(NZ, ROWS, HD)

    def own_rows_kv():
        both = g_own[pl.ds(1, 2)].reshape(2 * HD, TOK)
        value = dot_t(nrm_t[pl.ds(y * NZ, NZ)].reshape(NZ * ROWS, TOK), both)
        ctr[1] = value[:, :HD].reshape(NZ, ROWS, HD)
        ctr[2] = value[:, HD:].reshape(NZ, ROWS, HD)

    def norm_back(raw, gain, cotangent):
        scale = scale_of(raw)
        inner = gain * cotangent
        mixed = jnp.sum(raw * inner, axis=0, keepdims=True) * (1.0 / HD)
        return scale * inner - raw * (scale * scale * scale * mixed)

    def pair_tokens(g):
        return bpair if g == 3 else npair

    def pair_rows(g):
        value = dot_t(pair_tokens(g)[...].reshape(NZ * ROWS, TOK), g_pair[g])
        ctr[g] = ctr[g] + value.reshape(NZ, ROWS, HD)

    def pair_rows_kv():
        both = g_pair[pl.ds(1, 2)].reshape(2 * HD, TOK)
        value = dot_t(npair[...].reshape(NZ * ROWS, TOK), both)
        ctr[1] = ctr[1] + value[:, :HD].reshape(NZ, ROWS, HD)
        ctr[2] = ctr[2] + value[:, HD:].reshape(NZ, ROWS, HD)

    def term(g, k):
        return ctr[g, (z + k + NZ) % NZ]

    def stage(g, st):
        if st == 4:
            arrived("g%d" % g, g_pair.at[g])
            value = term(g, 4) + dot_t(pair_tokens(g)[(z + 4) % NZ], g_pair[g])
            value = value.astype(BF16)
            for d in (0, 1):
                rows = rows_of(d)
                ring_send[g, d, 3, rows, :] = value[HALF * d : HALF * (d + 1)]
                send(
                    "r%d%d4" % (g, d),
                    ring_send.at[g, d, 3, rows],
                    ring_in.at[g, d, 3, rows],
                    (up, down)[d],
                )
            return
        for d in (0, 1):
            value = term(g, st if d == 0 else -st)
            if st == 3:
                rows, rest = rows_of(d), rows_of(1 - d)
                arrived("r%d%d4" % (g, d), ring_in.at[g, d, 3, rows])
                ring_send[g, d, 2, rows, :] = (
                    value[HALF * d : HALF * (d + 1)] + ring_in[g, d, 3, rows, :].astype(F32)
                ).astype(BF16)
                ring_send[g, d, 2, rest, :] = value[HALF * (1 - d) : HALF * (2 - d)].astype(BF16)
            else:
                arrived("r%d%d%d" % (g, d, st + 1), ring_in.at[g, d, st])
                ring_send[g, d, st - 1] = (value + ring_in[g, d, st].astype(F32)).astype(BF16)
            send(
                "r%d%d%d" % (g, d, st),
                ring_send.at[g, d, st - 1],
                ring_in.at[g, d, st - 1],
                (up, down)[d],
            )

    def finish(g):
        value = term(g, 0)
        for d in (0, 1):
            arrived("r%d%d1" % (g, d), ring_in.at[g, d, 0])
            value = value + ring_in[g, d, 0].astype(F32)
        if g == 3:
            go_ref[...] = value
        else:
            gq_ref[:, g * HD : (g + 1) * HD] = value

    weight_grad(0)
    weight_grad(2)
    delta = jnp.zeros((1, TOK), F32)
    for col in range(3):
        delta = delta + jnp.sum(exps[col] * wgs[col], axis=0, keepdims=True)
    stats[2] = jnp.broadcast_to(delta, (8, TOK))
    halo_send("delta", stats.at[2], delta_at)
    for col in range(3):
        ds_b[col] = (exps[col] * (wgs[col] - delta)).astype(BF16)

    dq = (
        dot(kv[0, 0], ds_b[0]) + dot(kv[1, 0], ds_b[1]) + dot(kv[2, 0], ds_b[2])
    ) * head_scale
    g_own[0] = norm_back(acc[0:HD, :], gain_of(0), dq).astype(BF16)
    send("g0", g_own.at[0], g_pair.at[0], across)
    own_rows(3)
    halo_wait("dout", dout_at)
    halo_wait("q", q_at)
    halo_wait("stats", stats_at)
    keys = kv[1, 0].T
    values = kv[1, 1].T
    dk = dot_t(q_t[...], ds_b[1])
    dv = dot_t(dout_t[...], w_b[1])
    for side in (0, 1):
        score = dot(keys, q_in[side]) * head_scale
        exps[side] = jnp.exp(score - stats_in[side, 0, 0:1, :]) / stats_in[side, 1, 0:1, :]
        wgs[side] = dot(values, dout_in[side])
    for side in (0, 1):
        w_b[side] = exps[side].astype(BF16)
        dv = dv + dot_t(dout_in[side], w_b[side])
    g_own[2] = dv.astype(BF16)
    send("g2", g_own.at[2], g_pair.at[2], across)
    halo_wait("delta", delta_at)
    for side in (0, 1):
        ds_b[side] = (exps[side] * (wgs[side] - stats_in[side, 2, 0:1, :])).astype(BF16)
        dk = dk + dot_t(q_in[side], ds_b[side])
    g_own[1] = norm_back(acc[HD : 2 * HD, :], gain_of(1), dk * head_scale).astype(BF16)
    send("g1", g_own.at[1], g_pair.at[1], across)
    terms(0, False, ht_send)
    send("ht0", ht_send.at[0], ht_sib.at[0], sibling)
    for d in (0, 1, 2, 3):
        arrived("bpc%d" % d, bpair.at[bp_index(y, yh, (x + 4 - d) % 4, 1 - core)])
    stage(3, 4)
    terms(0, True, ht_own)
    own_rows(0)

    pair_rows(3)
    arrived("npc0", npair.at[m_core])
    for d in (1, 2, 3):
        arrived("npc%d" % d, npair.at[(m_core - 2 * d + 8) % 8])
    stage(0, 4)
    stage(3, 3)
    own_rows_kv()
    pair_rows(0)
    terms_sum(0)

    stage(1, 4)
    stage(2, 4)
    stage(0, 3)
    stage(3, 2)
    pair_rows_kv()
    terms(1, False, ht_send)
    send("ht1", ht_send.at[1], ht_sib.at[1], sibling)
    terms(1, True, ht_own)
    stage(1, 3)
    stage(0, 2)
    stage(2, 3)
    stage(3, 1)
    stage(1, 2)
    stage(0, 1)
    stage(2, 2)
    finish(3)

    terms_sum(1)
    stage(1, 1)
    finish(0)
    stage(2, 1)
    y_send[...] = x_sum(0).astype(BF16)
    send("by", y_send, y_in, y_far)
    finish(1)
    finish(2)
    near = x_sum(1)
    arrived("by", y_in)
    branch = (near + y_in[...].astype(F32)).astype(BF16)
    sample_ref[...] = (branch.astype(F32) + noise_level * noise_ref[...].astype(F32)).astype(BF16)
    for copy in sent:
        copy.wait_send()

    for name, src, landing in halo_sent:

        @pl.when(has_right)
        def _(name=name, src=src, landing=landing):
            copy_of(name + ">", src, landing(0), right).wait_send()

        @pl.when(has_left)
        def _(name=name, src=src, landing=landing):
            copy_of(name + "<", src, landing(1), left).wait_send()


def hand_over(a_ref, b_ref, c_ref, a_out, b_out, c_out):
    a_out[...] = a_ref[...]
    b_out[...] = b_ref[...]
    c_out[...] = c_ref[...]


def shards(hidden, noise, norm_gain, qk_gain, w_qkv, w_out, rewards):
    vmem = pl.BlockSpec(memory_space=pltpu.VMEM)
    anywhere = pl.BlockSpec(memory_space=pl.ANY)
    block = (ROWS, TOK)
    head = (HD, TOK)
    scratch = [
        pltpu.VMEM(hidden.shape, BF16),
        pltpu.VMEM(block, BF16),
        pltpu.VMEM((16, ROWS, 3 * HD), BF16),
        pltpu.VMEM((16, ROWS, HD), BF16),
        pltpu.VMEM((16, *block), BF16),
        pltpu.VMEM((8, *block), BF16),
        pltpu.VMEM((16, *block), BF16),
        pltpu.VMEM((8, *block), BF16),
        pltpu.VMEM((TOK, 128), F32),
        pltpu.VMEM((3 * HD, TOK), F32),
        pltpu.VMEM(head, F32),
        pltpu.VMEM(head, BF16),
        pltpu.VMEM(head, BF16),
        pltpu.VMEM((3, 2, *head), BF16),
        pltpu.VMEM((2, *head), BF16),
        pltpu.VMEM((2, *head), BF16),
        pltpu.VMEM((3, 8, TOK), F32),
        pltpu.VMEM((2, 3, 8, TOK), F32),
        pltpu.VMEM((3, TOK, TOK), F32),
        pltpu.VMEM((3, TOK, TOK), F32),
        pltpu.VMEM((3, TOK, TOK), BF16),
        pltpu.VMEM((3, TOK, TOK), BF16),
        pltpu.VMEM((2, 4, *block), BF16),
        pltpu.VMEM((2, 4, *block), BF16),
        pltpu.VMEM((2, 4, *block), BF16),
        pltpu.VMEM((2, 4, *block), BF16),
        pltpu.VMEM((2, 3, *block), BF16),
        pltpu.VMEM(block, BF16),
        pltpu.VMEM(block, BF16),
        pltpu.VMEM((4, *head), BF16),
        pltpu.VMEM((4, *head), BF16),
        pltpu.VMEM((4, 8, ROWS, HD), F32),
        pltpu.VMEM((4, 2, 4, ROWS, HD), BF16),
        pltpu.VMEM((4, 2, 4, ROWS, HD), BF16),
        pltpu.SemaphoreType.DMA((NSEM,)),
        pltpu.SemaphoreType.DMA((NSEM,)),
        pltpu.SemaphoreType.DMA((4,)),
    ]
    outs = (
        jax.ShapeDtypeStruct((ROWS, TOK), BF16),
        jax.ShapeDtypeStruct((ROWS, 3 * HD), F32),
        jax.ShapeDtypeStruct((ROWS, HD), F32),
    )
    results = pl.pallas_call(
        kernel,
        out_shape=outs,
        in_specs=[anywhere, anywhere, vmem, vmem, anywhere, anywhere, vmem],
        out_specs=(vmem, vmem, vmem),
        scratch_shapes=scratch,
        compiler_params=pltpu.CompilerParams(
            collective_id=0, has_side_effects=True, vmem_limit_bytes=56 * 1024 * 1024
        ),
    )(
        hidden,
        noise.T,
        norm_gain.reshape(1, -1),
        qk_gain,
        w_qkv,
        w_out,
        rewards.reshape(1, -1),
    )
    sample_t, grad_qkv, grad_out = pl.pallas_call(
        hand_over, out_shape=outs, in_specs=[vmem] * 3, out_specs=(vmem, vmem, vmem)
    )(*results)
    return sample_t.T, grad_qkv, grad_out


def solution(mesh):
    return jax.shard_map(
        shards,
        mesh=mesh,
        in_specs=(
            P("slab", None),
            P("slab", "fsdp"),
            P(),
            P(),
            P("slab", "fsdp"),
            P("slab", "fsdp"),
            P(),
        ),
        out_specs=(P("slab", "fsdp"), P("slab", "fsdp"), P("slab", "fsdp")),
        check_vma=False,
    )
```

time: 90.7 us -> 80.6 us (0.89)
  Pallas kernels: 89.6 us -> 79.8 us
    pallas_call x1, Pallas kernels: 87.8 us -> 77.9 us  [shards(): pl.pallas_call(kernel, out_shape=outs, in_specs=[anywhere, anywhere, vmem...]
where the time goes in v3:
time: 80.6 us; the launch traced here: 80.4 us
  Pallas kernels  79.8 us (99%)
    pallas_call x1, Pallas kernels, shards(): pl.pallas_call(kernel, out_shape=outs, in_specs=[anywhere, anywhere, vmem...  77.9 us
    pallas_call x1, Pallas kernels, shards(): pl.pallas_call(hand_over, out_shape=outs, in_specs=[vmem] * 3, out_specs=...  1.86 us

profile of v3, /device:TPU:2, one launch (start us, length us, event | category | flops | bytes accessed | tf_op | source)
XLA Modules:
  0.0 80.4 jit_solution(8210203576962432564)
XLA Ops:
  0.6 77.9 %shard_map.94 = (bf16[192,384]{1,0:T(8,128)(2,1)}, f32[192,384]{1,0:T(8,128)}, f32[192,128]{1,0:T(8,128)}) custom-call(bf16[384,3072]{1,0:T(8,128)(2,1)} %hidden_hbm.1, bf16[192,384]{1,0:T(8,128)(2,1)} %bitcast.4, f32[1,3072]{1,0:T(1,128)} %bitcast.5, f32[2,128]{1,0:T(2,128)} %qk_gain_ref.1, bf16[192,384]{1,0:T(8,128)(2,1)} %wq_hbm.1, ...), custom_call_target="tpu_custom_call" | custom-call | tf_op jit(solution)/shard_map/pallas_call | solution.py:688
  78.5 1.9 %shard_map.95 = (bf16[192,384]{1,0:T(8,128)(2,1)}, f32[192,384]{1,0:T(8,128)}, f32[192,128]{1,0:T(8,128)}) custom-call(bf16[192,384]{1,0:T(8,128)(2,1)} %get-tuple-element.9.a_ref, f32[192,384]{1,0:T(8,128)} %get-tuple-element.10.b_ref, f32[192,128]{1,0:T(8,128)} %get-tuple-element.11.c_ref), custom_call_target="tpu_custom_call" | custom-call | tf_op jit(solution)/shard_map/pallas_call | solution.py:706

commit v4 on v3

--- a/solution.py
+++ b/solution.py
@@ -33,13 +33,13 @@
 
 
 def kernel(
-    hidden_hbm, noise_hbm, gain_ref, qk_gain_ref, wq_hbm, wo_hbm, rewards_ref,
-    sample_ref, gq_ref, go_ref,
-    hidden_ref, noise_ref, wq, wo, bg, bpair, nrm_t, npair, row_scale, acc, dacc, q_t, dout_t,
+    hidden_hbm, noise_hbm, gain_hbm, qk_gain_hbm, wq_hbm, wo_hbm, rewards_hbm,
+    sample_hbm, gq_hbm, go_hbm,
+    hidden_ref, noise_ref, gain_ref, qk_gain_ref, rewards_ref, wq, wo, bg, bpair, nrm_t, npair, row_scale, acc, dacc, q_t, dout_t,
     kv, q_in, dout_in, stats, stats_in, exps, wgs, w_b, ds_b,
     ht_send, ht_own, ht_sib, part, part_in, y_send, y_in,
     g_own, g_pair, ctr, ring_send, ring_in,
-    ssem, rsem, hsem,
+    sample_ref, gq_ref, go_ref, ssem, rsem, hsem,
 ):
     s = lax.axis_index("slab")
     f = lax.axis_index("fsdp")
@@ -100,31 +100,30 @@
     wq_copy = pltpu.make_async_copy(wq_hbm, wq.at[s], hsem.at[1])
     wo_copy = pltpu.make_async_copy(wo_hbm, wo.at[s], hsem.at[2])
     hidden_copy = pltpu.make_async_copy(hidden_hbm, hidden_ref, hsem.at[3])
-    for copy in (noise_copy, wq_copy, wo_copy, hidden_copy):
+    gain_copy = pltpu.make_async_copy(gain_hbm, gain_ref, hsem.at[9])
+    qk_gain_copy = pltpu.make_async_copy(qk_gain_hbm, qk_gain_ref, hsem.at[10])
+    rewards_copy = pltpu.make_async_copy(rewards_hbm, rewards_ref, hsem.at[11])
+    for copy in (
+        rewards_copy, noise_copy, wq_copy, wo_copy, hidden_copy, gain_copy, qk_gain_copy
+    ):
         copy.start()
 
-    rewards = rewards_ref[...]
-    advantage = rewards[:, 0:1] - jnp.sum(rewards, axis=1, keepdims=True) * (1.0 / rewards.shape[1])
-    factor = -advantage / noise_level
-    noise_copy.wait()
-    bg[f] = (noise_ref[...].astype(F32) * factor).astype(BF16)
-    wq_copy.wait()
-    wo_copy.wait()
-
-    pl.semaphore_wait(barrier, len(partners))
-
     halo_sent = []
 
-    def halo_send(name, src, landing):
-        @pl.when(has_right)
+    def halo_send(name, src, landing, only=None):
+        right_too = has_right if only is None else jnp.logical_and(has_right, core == only)
+        left_too = has_left if only is None else jnp.logical_and(has_left, core == only)
+
+        @pl.when(right_too)
         def _():
             copy_of(name + ">", src, landing(0), right).start()
 
-        @pl.when(has_left)
+        @pl.when(left_too)
         def _():
             copy_of(name + "<", src, landing(1), left).start()
 
-        halo_sent.append((name, src, landing))
+        if only != 1:
+            halo_sent.append((name, src, landing))
 
     def halo_wait(name, landing):
         @pl.when(has_left)
@@ -165,8 +164,8 @@
 
     def q_start():
         for i in (0, 1):
-            send("qu%d" % i, q_piece(0, 0, i), q_piece(0, 0, i), up)
-            send("qd%d" % i, q_piece(0, 0, 1 - i), q_piece(0, 0, 1 - i), down)
+            send("qu%d" % i, wq_hbm.at[rows_of(i)], q_piece(0, 0, i), up)
+            send("qd%d" % i, wq_hbm.at[rows_of(1 - i)], q_piece(0, 0, 1 - i), down)
 
     def q_event(n):
         flip, k, second = incoming[n]
@@ -192,9 +191,9 @@
 
     def o_start():
         block = wo.at[s]
-        send("ou0", block, block, up)
-        send("od0", block, block, down)
-        send("oa0", block, block, across)
+        send("ou0", wo_hbm, block, up)
+        send("od0", wo_hbm, block, down)
+        send("oa0", wo_hbm, block, across)
 
     def o_event(n):
         for i, (link, sign, h, to) in enumerate((("ou", -1, 0, up), ("od", 1, 1, down))):
@@ -223,7 +222,16 @@
             j = slab(flip, k)
             acc[...] += dot_first(wq[j], nrm_t[j])
 
+    pl.semaphore_wait(barrier, len(partners))
+
     q_start()
+    rewards_copy.wait()
+    rewards = rewards_ref[...]
+    advantage = rewards[:, 0:1] - jnp.sum(rewards, axis=1, keepdims=True) * (1.0 / rewards.shape[1])
+    factor = -advantage / noise_level
+    noise_copy.wait()
+    bg[f] = (noise_ref[...].astype(F32) * factor).astype(BF16)
+
 
     f_y = f + 2 - 4 * yh
 
@@ -238,8 +246,10 @@
     pass_bg("nx-", f, x_dev(3))
     pass_bg("nc", f, sibling)
     o_start()
+
     hidden_copy.wait()
-
+    gain_copy.wait()
+    qk_gain_copy.wait()
     def scales(i, carry):
         rows = pl.ds(pl.multiple_of(i * 48, 16), 48)
         values = hidden_ref[rows, :].astype(F32)
@@ -267,6 +277,7 @@
     m_core = 2 * x + 1 - core
     send("np", nrm_t.at[(1 - y) * NZ + m], npair.at[m], beyond)
     o_event(0)
+    wq_copy.wait()
     project((0, 0))
     arrived("nx+", bg.at[block_x(f, -1)])
     pass_bg("nx2", block_x(f, -1), x_dev(1))
@@ -285,14 +296,11 @@
     send("bp", bg.at[(1 - y) * NZ + b_out], bpair.at[b_out], beyond)
     q_event(2)
     project((0, -1), (0, 1))
+    q_across(0, 7)
     q_event(3)
-    for i in (0, 1):
-        send("qa%d" % i, q_piece(0, 0, i), q_piece(0, 0, i), across)
     o_event(1)
     q_event(4)
-    q_across(0, 7)
     project((0, -2), (0, 2))
-    q_event(5)
     arrived("yx-", bg.at[block_x(f_y, 1)])
     pass_bg("yx2", block_x(f_y, 1), x_dev(3))
     pass_bg("yc3", block_x(f_y, 1), sibling)
@@ -300,29 +308,32 @@
     pass_bg("yc1", block_x(f_y, -1), sibling)
     arrived("nx2", bg.at[block_x(f, 2)])
     pass_bg("nc2", block_x(f, 2), sibling)
-    o_event(2)
-    q_across(1, None)
-    project((0, -3), (0, 3))
-    q_event(6)
-    o_event(3)
-    arrived("np", npair.at[m])
-    for d in (1, 2, 3):
-        send("np%d" % d, npair.at[m], npair.at[m], x_dev(d))
-    send("npc0", npair.at[m], npair.at[m], sibling)
-    project((0, 4), (1, -1), (1, 1))
     q_event(7)
+    q_event(5)
     q_across(3, 9)
-    project((1, -2), (1, 2))
-    q_event(8)
-    arrived("yx2", bg.at[block_x(f_y, 2)])
-    pass_bg("yc2", block_x(f_y, 2), sibling)
-    q_across_own()
-    q_event(9)
+    for i in (0, 1):
+        send("qa%d" % i, wq_hbm.at[rows_of(i)], q_piece(0, 0, i), across)
     b_in = bp_index(y, yh, x, core)
     arrived("bp", bpair.at[b_in])
     for d in (1, 2, 3):
         send("bp%d" % d, bpair.at[b_in], bpair.at[b_in], x_dev(d))
     send("bpc0", bpair.at[b_in], bpair.at[b_in], sibling)
+    arrived("np", npair.at[m])
+    for d in (1, 2, 3):
+        send("np%d" % d, npair.at[m], npair.at[m], x_dev(d))
+    send("npc0", npair.at[m], npair.at[m], sibling)
+    o_event(2)
+    q_event(8)
+    q_across(1, None)
+    project((0, -3), (0, 3))
+    q_event(6)
+    o_event(3)
+    project((0, 4), (1, -1), (1, 1))
+    project((1, -2), (1, 2))
+    q_event(9)
+    arrived("yx2", bg.at[block_x(f_y, 2)])
+    pass_bg("yc2", block_x(f_y, 2), sibling)
+    q_across_own()
     project((1, -3), (1, 3), (1, 0))
     def out_grad(*blocks):
         total = dacc[...]
@@ -385,6 +396,7 @@
     arrived("yc3", bg.at[block_x(f_ycore, 1)])
     arrived("yc2", bg.at[block_x(f_ycore, 2)])
 
+    wo_copy.wait()
     out_grad((0, 0), (0, -1), (0, 1), (0, -2), (0, 2))
     o_across(0)
     o_across(1)
@@ -396,17 +408,13 @@
     o_across(4)
     out_grad((1, 4))
     dout_t[...] = dacc[...].astype(BF16)
-    halo_send("dout", dout_t, dout_at)
-    halo_send("q", q_t, q_at)
-    for d in (1, 2, 3):
-        chunk = npair.at[(m - 2 * d + 8) % 8]
-        arrived("np%d" % d, chunk)
-        send("npc%d" % d, chunk, chunk, sibling)
+    halo_send("dout", dout_t, dout_at, 0)
+    halo_send("q", q_t, q_at, 0)
+    weight_grad(1)
     for d in (1, 2, 3):
         chunk = bpair.at[bp_index(y, yh, (x + 4 - d) % 4, core)]
         arrived("bp%d" % d, chunk)
         send("bpc%d" % d, chunk, chunk, sibling)
-    weight_grad(1)
     halo_wait("k", k_at)
     peak = jnp.maximum(peak, scores(0))
     peak = jnp.maximum(peak, scores(2))
@@ -422,11 +430,12 @@
         value = exps[col] / total
         exps[col] = value
         w_b[col] = value.astype(BF16)
+    halo_send("dout", dout_t, dout_at, 1)
     halo_wait("v", v_at)
     attended = dot(kv[0, 1], w_b[0]) + dot(kv[1, 1], w_b[1]) + dot(kv[2, 1], w_b[2])
     g_own[3] = attended.astype(BF16)
-    send("g3", g_own.at[3], g_pair.at[3], across)
-
+
+    halo_send("q", q_t, q_at, 1)
     def terms(phase, own, buf):
         h = 1 - yh if phase == 0 else yh
         c = core if own else 1 - core
@@ -454,35 +463,34 @@
             value = value + part_in[phase, d - 1].astype(F32)
         return value
 
-    def own_rows(g):
-        tokens = bg if g == 3 else nrm_t
-        value = dot_t(tokens[pl.ds(y * NZ, NZ)].reshape(NZ * ROWS, TOK), g_own[g])
-        ctr[g] = value.reshape(NZ, ROWS, HD)
-
-    def own_rows_kv():
-        both = g_own[pl.ds(1, 2)].reshape(2 * HD, TOK)
-        value = dot_t(nrm_t[pl.ds(y * NZ, NZ)].reshape(NZ * ROWS, TOK), both)
-        ctr[1] = value[:, :HD].reshape(NZ, ROWS, HD)
-        ctr[2] = value[:, HD:].reshape(NZ, ROWS, HD)
-
     def norm_back(raw, gain, cotangent):
         scale = scale_of(raw)
         inner = gain * cotangent
         mixed = jnp.sum(raw * inner, axis=0, keepdims=True) * (1.0 / HD)
         return scale * inner - raw * (scale * scale * scale * mixed)
 
+    handed = []
+
+    def hand_out(src, dst):
+        copy = pltpu.make_async_copy(src, dst, hsem.at[4 + len(handed)])
+        copy.start()
+        handed.append(copy)
+
+    def tokens_of(g):
+        return bg if g == 3 else nrm_t
+
     def pair_tokens(g):
         return bpair if g == 3 else npair
 
-    def pair_rows(g):
-        value = dot_t(pair_tokens(g)[...].reshape(NZ * ROWS, TOK), g_pair[g])
-        ctr[g] = ctr[g] + value.reshape(NZ, ROWS, HD)
-
-    def pair_rows_kv():
-        both = g_pair[pl.ds(1, 2)].reshape(2 * HD, TOK)
-        value = dot_t(npair[...].reshape(NZ * ROWS, TOK), both)
-        ctr[1] = ctr[1] + value[:, :HD].reshape(NZ, ROWS, HD)
-        ctr[2] = ctr[2] + value[:, HD:].reshape(NZ, ROWS, HD)
+    def rows_sum(*groups):
+        first, count = groups[0], len(groups)
+        own = g_own[pl.ds(first, count)].reshape(count * HD, TOK)
+        pair = g_pair[pl.ds(first, count)].reshape(count * HD, TOK)
+        value = dot_t(
+            tokens_of(first)[pl.ds(y * NZ, NZ)].reshape(NZ * ROWS, TOK), own
+        ) + dot_t(pair_tokens(first)[...].reshape(NZ * ROWS, TOK), pair)
+        for i, g in enumerate(groups):
+            ctr[g] = value[:, i * HD : (i + 1) * HD].reshape(NZ, ROWS, HD)
 
     def term(g, k):
         return ctr[g, (z + k + NZ) % NZ]
@@ -490,7 +498,8 @@
     def stage(g, st):
         if st == 4:
             arrived("g%d" % g, g_pair.at[g])
-            value = term(g, 4) + dot_t(pair_tokens(g)[(z + 4) % NZ], g_pair[g])
+            zd = (z + 4) % NZ
+            value = dot_t(tokens_of(g)[y * NZ + zd], g_own[g]) + dot_t(pair_tokens(g)[zd], g_pair[g])
             value = value.astype(BF16)
             for d in (0, 1):
                 rows = rows_of(d)
@@ -528,8 +537,11 @@
             value = value + ring_in[g, d, 0].astype(F32)
         if g == 3:
             go_ref[...] = value
+            hand_out(go_ref, go_hbm)
         else:
-            gq_ref[:, g * HD : (g + 1) * HD] = value
+            cols = pl.ds(g * HD, HD)
+            gq_ref[:, cols] = value
+            hand_out(gq_ref.at[:, cols], gq_hbm.at[:, cols])
 
     weight_grad(0)
     weight_grad(2)
@@ -546,7 +558,14 @@
     ) * head_scale
     g_own[0] = norm_back(acc[0:HD, :], gain_of(0), dq).astype(BF16)
     send("g0", g_own.at[0], g_pair.at[0], across)
-    own_rows(3)
+    send("g3", g_own.at[3], g_pair.at[3], across)
+    for d in (1, 2, 3):
+        chunk = npair.at[(m - 2 * d + 8) % 8]
+        arrived("np%d" % d, chunk)
+        send("npc%d" % d, chunk, chunk, sibling)
+    terms(0, False, ht_send)
+    send("ht0", ht_send.at[0], ht_sib.at[0], sibling)
+    terms(0, True, ht_own)
     halo_wait("dout", dout_at)
     halo_wait("q", q_at)
     halo_wait("stats", stats_at)
@@ -569,53 +588,50 @@
         dk = dk + dot_t(q_in[side], ds_b[side])
     g_own[1] = norm_back(acc[HD : 2 * HD, :], gain_of(1), dk * head_scale).astype(BF16)
     send("g1", g_own.at[1], g_pair.at[1], across)
-    terms(0, False, ht_send)
-    send("ht0", ht_send.at[0], ht_sib.at[0], sibling)
-    for d in (0, 1, 2, 3):
-        arrived("bpc%d" % d, bpair.at[bp_index(y, yh, (x + 4 - d) % 4, 1 - core)])
-    stage(3, 4)
-    terms(0, True, ht_own)
-    own_rows(0)
-
-    pair_rows(3)
     arrived("npc0", npair.at[m_core])
     for d in (1, 2, 3):
         arrived("npc%d" % d, npair.at[(m_core - 2 * d + 8) % 8])
     stage(0, 4)
-    stage(3, 3)
-    own_rows_kv()
-    pair_rows(0)
+    for d in (0, 1, 2, 3):
+        arrived("bpc%d" % d, bpair.at[bp_index(y, yh, (x + 4 - d) % 4, 1 - core)])
+    stage(3, 4)
     terms_sum(0)
 
-    stage(1, 4)
-    stage(2, 4)
-    stage(0, 3)
-    stage(3, 2)
-    pair_rows_kv()
     terms(1, False, ht_send)
     send("ht1", ht_send.at[1], ht_sib.at[1], sibling)
     terms(1, True, ht_own)
+    rows_sum(0)
+    stage(2, 4)
+    stage(1, 4)
+    rows_sum(3)
+    stage(0, 3)
+    stage(3, 3)
+    rows_sum(1, 2)
+    stage(2, 3)
     stage(1, 3)
+    terms_sum(1)
     stage(0, 2)
-    stage(2, 3)
-    stage(3, 1)
+    stage(3, 2)
+    stage(2, 2)
     stage(1, 2)
     stage(0, 1)
-    stage(2, 2)
-    finish(3)
-
-    terms_sum(1)
+    stage(3, 1)
+    y_send[...] = x_sum(0).astype(BF16)
+    send("by", y_send, y_in, y_far)
+    stage(2, 1)
     stage(1, 1)
     finish(0)
-    stage(2, 1)
-    y_send[...] = x_sum(0).astype(BF16)
-    send("by", y_send, y_in, y_far)
+    finish(3)
+
+    finish(2)
     finish(1)
-    finish(2)
     near = x_sum(1)
     arrived("by", y_in)
     branch = (near + y_in[...].astype(F32)).astype(BF16)
     sample_ref[...] = (branch.astype(F32) + noise_level * noise_ref[...].astype(F32)).astype(BF16)
+    hand_out(sample_ref, sample_hbm)
+    for copy in handed:
+        copy.wait()
     for copy in sent:
         copy.wait_send()
 
@@ -644,6 +660,9 @@
     scratch = [
         pltpu.VMEM(hidden.shape, BF16),
         pltpu.VMEM(block, BF16),
+        pltpu.VMEM((1, hidden.shape[1]), F32),
+        pltpu.VMEM(qk_gain.shape, F32),
+        pltpu.VMEM((1, rewards.shape[0]), F32),
         pltpu.VMEM((16, ROWS, 3 * HD), BF16),
         pltpu.VMEM((16, ROWS, HD), BF16),
         pltpu.VMEM((16, *block), BF16),
@@ -676,9 +695,12 @@
         pltpu.VMEM((4, 8, ROWS, HD), F32),
         pltpu.VMEM((4, 2, 4, ROWS, HD), BF16),
         pltpu.VMEM((4, 2, 4, ROWS, HD), BF16),
+        pltpu.VMEM(block, BF16),
+        pltpu.VMEM((ROWS, 3 * HD), F32),
+        pltpu.VMEM((ROWS, HD), F32),
         pltpu.SemaphoreType.DMA((NSEM,)),
         pltpu.SemaphoreType.DMA((NSEM,)),
-        pltpu.SemaphoreType.DMA((4,)),
+        pltpu.SemaphoreType.DMA((12,)),
     ]
     outs = (
         jax.ShapeDtypeStruct((ROWS, TOK), BF16),
@@ -688,8 +710,8 @@
     results = pl.pallas_call(
         kernel,
         out_shape=outs,
-        in_specs=[anywhere, anywhere, vmem, vmem, anywhere, anywhere, vmem],
-        out_specs=(vmem, vmem, vmem),
+        in_specs=[anywhere] * 7,
+        out_specs=(anywhere, anywhere, anywhere),
         scratch_shapes=scratch,
         compiler_params=pltpu.CompilerParams(
             collective_id=0, has_side_effects=True, vmem_limit_bytes=56 * 1024 * 1024

time: 80.6 us -> 75.7 us (0.939)
  Pallas kernels: 79.8 us -> 74.1 us
    pallas_call x1, Pallas kernels: 77.9 us -> 72.2 us  [shards(): pl.pallas_call(kernel, out_shape=outs, in_specs=[anywhere] * 7, out_specs...]
where the time goes in v4:
time: 75.7 us; the launch traced here: 74.7 us
  Pallas kernels  74.1 us (98%)
    pallas_call x1, Pallas kernels, shards(): pl.pallas_call(kernel, out_shape=outs, in_specs=[anywhere] * 7, out_specs...  72.2 us
    pallas_call x1, Pallas kernels, shards(): pl.pallas_call(hand_over, out_shape=outs, in_specs=[vmem] * 3, out_specs=...  1.86 us

profile of v4, /device:TPU:2, one launch (start us, length us, event | category | flops | bytes accessed | tf_op | source)
XLA Modules:
  0.0 74.7 jit_solution(4686494870738684998)
XLA Ops:
  0.6 72.2 %shard_map.94 = (bf16[192,384]{1,0:T(8,128)(2,1)}, f32[192,384]{1,0:T(8,128)}, f32[192,128]{1,0:T(8,128)}) custom-call(bf16[384,3072]{1,0:T(8,128)(2,1)} %hidden_hbm.1, bf16[192,384]{1,0:T(8,128)(2,1)} %bitcast.4, f32[1,3072]{1,0:T(1,128)} %bitcast.5, f32[2,128]{1,0:T(2,128)} %qk_gain_hbm.1, bf16[192,384]{1,0:T(8,128)(2,1)} %wq_hbm.1, ...), custom_call_target="tpu_custom_call" | custom-call | tf_op jit(solution)/shard_map/pallas_call | solution.py:710
  72.9 1.9 %shard_map.95 = (bf16[192,384]{1,0:T(8,128)(2,1)}, f32[192,384]{1,0:T(8,128)}, f32[192,128]{1,0:T(8,128)}) custom-call(bf16[192,384]{1,0:T(8,128)(2,1)} %get-tuple-element.9.a_ref, f32[192,384]{1,0:T(8,128)} %get-tuple-element.10.b_ref, f32[192,128]{1,0:T(8,128)} %get-tuple-element.11.c_ref), custom_call_target="tpu_custom_call" | custom-call | tf_op jit(solution)/shard_map/pallas_call | solution.py:728

commit v5 on v4

--- a/solution.py
+++ b/solution.py
@@ -34,12 +34,12 @@
 
 def kernel(
     hidden_hbm, noise_hbm, gain_hbm, qk_gain_hbm, wq_hbm, wo_hbm, rewards_hbm,
-    sample_hbm, gq_hbm, go_hbm,
+    sample_ref, gq_ref, go_ref,
     hidden_ref, noise_ref, gain_ref, qk_gain_ref, rewards_ref, wq, wo, bg, bpair, nrm_t, npair, row_scale, acc, dacc, q_t, dout_t,
     kv, q_in, dout_in, stats, stats_in, exps, wgs, w_b, ds_b,
     ht_send, ht_own, ht_sib, part, part_in, y_send, y_in,
     g_own, g_pair, ctr, ring_send, ring_in,
-    sample_ref, gq_ref, go_ref, ssem, rsem, hsem,
+    ssem, rsem, hsem,
 ):
     s = lax.axis_index("slab")
     f = lax.axis_index("fsdp")
@@ -469,13 +469,6 @@
         mixed = jnp.sum(raw * inner, axis=0, keepdims=True) * (1.0 / HD)
         return scale * inner - raw * (scale * scale * scale * mixed)
 
-    handed = []
-
-    def hand_out(src, dst):
-        copy = pltpu.make_async_copy(src, dst, hsem.at[4 + len(handed)])
-        copy.start()
-        handed.append(copy)
-
     def tokens_of(g):
         return bg if g == 3 else nrm_t
 
@@ -537,11 +530,9 @@
             value = value + ring_in[g, d, 0].astype(F32)
         if g == 3:
             go_ref[...] = value
-            hand_out(go_ref, go_hbm)
         else:
             cols = pl.ds(g * HD, HD)
             gq_ref[:, cols] = value
-            hand_out(gq_ref.at[:, cols], gq_hbm.at[:, cols])
 
     weight_grad(0)
     weight_grad(2)
@@ -629,9 +620,6 @@
     arrived("by", y_in)
     branch = (near + y_in[...].astype(F32)).astype(BF16)
     sample_ref[...] = (branch.astype(F32) + noise_level * noise_ref[...].astype(F32)).astype(BF16)
-    hand_out(sample_ref, sample_hbm)
-    for copy in handed:
-        copy.wait()
     for copy in sent:
         copy.wait_send()
 
@@ -646,10 +634,13 @@
             copy_of(name + "<", src, landing(1), left).wait_send()
 
 
-def hand_over(a_ref, b_ref, c_ref, a_out, b_out, c_out):
-    a_out[...] = a_ref[...]
-    b_out[...] = b_ref[...]
-    c_out[...] = c_ref[...]
+def hand_over(a_ref, b_ref, c_ref, a_out, b_out, c_out, sems):
+    pairs = ((b_ref, b_out), (a_ref, a_out), (c_ref, c_out))
+    copies = [pltpu.make_async_copy(src, dst, sems.at[i]) for i, (src, dst) in enumerate(pairs)]
+    for copy in copies:
+        copy.start()
+    for copy in copies:
+        copy.wait()
 
 
 def shards(hidden, noise, norm_gain, qk_gain, w_qkv, w_out, rewards):
@@ -695,9 +686,6 @@
         pltpu.VMEM((4, 8, ROWS, HD), F32),
         pltpu.VMEM((4, 2, 4, ROWS, HD), BF16),
         pltpu.VMEM((4, 2, 4, ROWS, HD), BF16),
-        pltpu.VMEM(block, BF16),
-        pltpu.VMEM((ROWS, 3 * HD), F32),
-        pltpu.VMEM((ROWS, HD), F32),
         pltpu.SemaphoreType.DMA((NSEM,)),
         pltpu.SemaphoreType.DMA((NSEM,)),
         pltpu.SemaphoreType.DMA((12,)),
@@ -709,9 +697,9 @@
     )
     results = pl.pallas_call(
         kernel,
-        out_shape=outs,
+        out_shape=tuple(pltpu.VMEM(out.shape, out.dtype) for out in outs),
         in_specs=[anywhere] * 7,
-        out_specs=(anywhere, anywhere, anywhere),
+        out_specs=(vmem, vmem, vmem),
         scratch_shapes=scratch,
         compiler_params=pltpu.CompilerParams(
             collective_id=0, has_side_effects=True, vmem_limit_bytes=56 * 1024 * 1024
@@ -726,8 +714,12 @@
         rewards.reshape(1, -1),
     )
     sample_t, grad_qkv, grad_out = pl.pallas_call(
-        hand_over, out_shape=outs, in_specs=[vmem] * 3, out_specs=(vmem, vmem, vmem)
-    )(*results)
+        hand_over,
+        out_shape=outs,
+        in_specs=[vmem] * 3,
+        out_specs=(anywhere, anywhere, anywhere),
+        scratch_shapes=[pltpu.SemaphoreType.DMA((3,))],
+    )(*(pltpu.with_memory_space_constraint(r, pltpu.VMEM) for r in results))
     return sample_t.T, grad_qkv, grad_out
 
 

time: 75.7 us -> 74.2 us (0.980)
  Pallas kernels: 74.1 us -> 72.4 us
    pallas_call x1, Pallas kernels: 1.86 us -> 0.82 us  [shards(): pl.pallas_call(hand_over, out_shape=outs, in_specs=[vmem] * 3, out_specs=...]
where the time goes in v5:
time: 74.2 us; the launch traced here: 73.2 us
  Pallas kernels  72.4 us (98%)
  between operations  0.8 us (1%)
    pallas_call x1, Pallas kernels, shards(): pl.pallas_call(kernel, out_shape=tuple((pltpu.VMEM(out.shape, out.dtype)...  71.6 us

profile of v5, /device:TPU:2, one launch (start us, length us, event | category | flops | bytes accessed | tf_op | source)
XLA Modules:
  0.0 73.2 jit_solution(5698392343096724300)
XLA Ops:
  0.6 71.6 %shard_map.94 = (bf16[192,384]{1,0:T(8,128)(2,1)S(1)}, f32[192,384]{1,0:T(8,128)S(1)}, f32[192,128]{1,0:T(8,128)S(1)}) custom-call(bf16[384,3072]{1,0:T(8,128)(2,1)} %hidden_hbm.1, bf16[192,384]{1,0:T(8,128)(2,1)} %bitcast.4, f32[1,3072]{1,0:T(1,128)} %bitcast.5, f32[2,128]{1,0:T(2,128)} %qk_gain_hbm.1, bf16[192,384]{1,0:T(8,128)(2,1)} %wq_hbm.1, ...), custom_call_target="tpu_custom_call" | custom-call | tf_op jit(solution)/shard_map/pallas_call | solution.py:698
  72.2 0.8 %shard_map.95 = (bf16[192,384]{1,0:T(8,128)(2,1)}, f32[192,384]{1,0:T(8,128)}, f32[192,128]{1,0:T(8,128)}) custom-call(bf16[192,384]{1,0:T(8,128)(2,1)S(1)} %get-tuple-element.9.a_ref, f32[192,384]{1,0:T(8,128)S(1)} %get-tuple-element.10.b_ref, f32[192,128]{1,0:T(8,128)S(1)} %get-tuple-element.11.c_ref), custom_call_target="tpu_custom_call" | custom-call | tf_op jit(solution)/shard_map/pallas_call | solution.py:716

commit v6 on v5

--- a/solution.py
+++ b/solution.py
@@ -475,15 +475,14 @@
     def pair_tokens(g):
         return bpair if g == 3 else npair
 
-    def rows_sum(*groups):
+    def rows_sum(pair, *groups):
         first, count = groups[0], len(groups)
-        own = g_own[pl.ds(first, count)].reshape(count * HD, TOK)
-        pair = g_pair[pl.ds(first, count)].reshape(count * HD, TOK)
-        value = dot_t(
-            tokens_of(first)[pl.ds(y * NZ, NZ)].reshape(NZ * ROWS, TOK), own
-        ) + dot_t(pair_tokens(first)[...].reshape(NZ * ROWS, TOK), pair)
+        grads = (g_pair if pair else g_own)[pl.ds(first, count)].reshape(count * HD, TOK)
+        tokens = pair_tokens(first)[...] if pair else tokens_of(first)[pl.ds(y * NZ, NZ)]
+        value = dot_t(tokens.reshape(NZ * ROWS, TOK), grads)
         for i, g in enumerate(groups):
-            ctr[g] = value[:, i * HD : (i + 1) * HD].reshape(NZ, ROWS, HD)
+            block = value[:, i * HD : (i + 1) * HD].reshape(NZ, ROWS, HD)
+            ctr[g] = ctr[g] + block if pair else block
 
     def term(g, k):
         return ctr[g, (z + k + NZ) % NZ]
@@ -549,7 +548,6 @@
     ) * head_scale
     g_own[0] = norm_back(acc[0:HD, :], gain_of(0), dq).astype(BF16)
     send("g0", g_own.at[0], g_pair.at[0], across)
-    send("g3", g_own.at[3], g_pair.at[3], across)
     for d in (1, 2, 3):
         chunk = npair.at[(m - 2 * d + 8) % 8]
         arrived("np%d" % d, chunk)
@@ -579,44 +577,48 @@
         dk = dk + dot_t(q_in[side], ds_b[side])
     g_own[1] = norm_back(acc[HD : 2 * HD, :], gain_of(1), dk * head_scale).astype(BF16)
     send("g1", g_own.at[1], g_pair.at[1], across)
+    send("g3", g_own.at[3], g_pair.at[3], across)
     arrived("npc0", npair.at[m_core])
     for d in (1, 2, 3):
         arrived("npc%d" % d, npair.at[(m_core - 2 * d + 8) % 8])
+    rows_sum(False, 0)
     stage(0, 4)
+    terms_sum(0)
+
+    terms(1, False, ht_send)
+    send("ht1", ht_send.at[1], ht_sib.at[1], sibling)
+    terms(1, True, ht_own)
+    rows_sum(True, 0)
+    rows_sum(False, 1, 2)
+    stage(2, 4)
+    rows_sum(False, 3)
+    stage(1, 4)
     for d in (0, 1, 2, 3):
         arrived("bpc%d" % d, bpair.at[bp_index(y, yh, (x + 4 - d) % 4, 1 - core)])
     stage(3, 4)
-    terms_sum(0)
-
-    terms(1, False, ht_send)
-    send("ht1", ht_send.at[1], ht_sib.at[1], sibling)
-    terms(1, True, ht_own)
-    rows_sum(0)
-    stage(2, 4)
-    stage(1, 4)
-    rows_sum(3)
     stage(0, 3)
-    stage(3, 3)
-    rows_sum(1, 2)
+    rows_sum(True, 1, 2)
     stage(2, 3)
     stage(1, 3)
+    rows_sum(True, 3)
     terms_sum(1)
+    stage(3, 3)
     stage(0, 2)
-    stage(3, 2)
     stage(2, 2)
     stage(1, 2)
-    stage(0, 1)
-    stage(3, 1)
     y_send[...] = x_sum(0).astype(BF16)
     send("by", y_send, y_in, y_far)
+    stage(3, 2)
+    stage(0, 1)
     stage(2, 1)
     stage(1, 1)
+    stage(3, 1)
     finish(0)
-    finish(3)
-
     finish(2)
     finish(1)
     near = x_sum(1)
+    finish(3)
+
     arrived("by", y_in)
     branch = (near + y_in[...].astype(F32)).astype(BF16)
     sample_ref[...] = (branch.astype(F32) + noise_level * noise_ref[...].astype(F32)).astype(BF16)

time: 74.2 us -> 73.1 us (0.985)
  Pallas kernels: 72.4 us -> 71.5 us
    pallas_call x1, Pallas kernels: 71.6 us -> 70.7 us  [shards(): pl.pallas_call(kernel, out_shape=tuple((pltpu.VMEM(out.shape, out.dtype)...]
where the time goes in v6:
time: 73.1 us; the launch traced here: 72.3 us
  Pallas kernels  71.5 us (98%)
  between operations  0.8 us (1%)
    pallas_call x1, Pallas kernels, shards(): pl.pallas_call(kernel, out_shape=tuple((pltpu.VMEM(out.shape, out.dtype)...  70.7 us

profile of v6, /device:TPU:2, one launch (start us, length us, event | category | flops | bytes accessed | tf_op | source)
XLA Modules:
  0.0 72.3 jit_solution(5059633727687200344)
XLA Ops:
  0.6 70.7 %shard_map.94 = (bf16[192,384]{1,0:T(8,128)(2,1)S(1)}, f32[192,384]{1,0:T(8,128)S(1)}, f32[192,128]{1,0:T(8,128)S(1)}) custom-call(bf16[384,3072]{1,0:T(8,128)(2,1)} %hidden_hbm.1, bf16[192,384]{1,0:T(8,128)(2,1)} %bitcast.4, f32[1,3072]{1,0:T(1,128)} %bitcast.5, f32[2,128]{1,0:T(2,128)} %qk_gain_hbm.1, bf16[192,384]{1,0:T(8,128)(2,1)} %wq_hbm.1, ...), custom_call_target="tpu_custom_call" | custom-call | tf_op jit(solution)/shard_map/pallas_call | solution.py:700
  71.4 0.8 %shard_map.95 = (bf16[192,384]{1,0:T(8,128)(2,1)}, f32[192,384]{1,0:T(8,128)}, f32[192,128]{1,0:T(8,128)}) custom-call(bf16[192,384]{1,0:T(8,128)(2,1)S(1)} %get-tuple-element.9.a_ref, f32[192,384]{1,0:T(8,128)S(1)} %get-tuple-element.10.b_ref, f32[192,128]{1,0:T(8,128)S(1)} %get-tuple-element.11.c_ref), custom_call_target="tpu_custom_call" | custom-call | tf_op jit(solution)/shard_map/pallas_call | solution.py:718

commit v7 on v6

--- a/solution.py
+++ b/solution.py
@@ -55,6 +55,8 @@
 
     up = (slab(0, 1), f)
     down = (slab(0, -1), f)
+    up2 = (slab(0, 2), f)
+    down2 = (slab(0, -2), f)
     across = (slab(1, 0), f)
     sibling = (s, f + 1 - 2 * core)
     y_far = (s, f + 2 - 4 * yh)
@@ -93,7 +95,7 @@
         copy_of(name, dst, dst, up).wait_recv()
 
     barrier = pltpu.get_barrier_semaphore()
-    partners = [up, down, across, sibling, y_far, x_dev(1), x_dev(2), x_dev(3), left, right, beyond]
+    partners = [up, down, across, sibling, y_far, x_dev(1), x_dev(2), x_dev(3), left, right, beyond, up2, down2]
     for to in partners:
         pl.semaphore_signal(barrier, inc=1, device_id=to, device_id_type=MESH)
     noise_copy = pltpu.make_async_copy(noise_hbm, noise_ref, hsem.at[0])
@@ -487,6 +489,8 @@
     def term(g, k):
         return ctr[g, (z + k + NZ) % NZ]
 
+    early = (0, 3)
+
     def stage(g, st):
         if st == 4:
             arrived("g%d" % g, g_pair.at[g])
@@ -500,21 +504,27 @@
                     "r%d%d4" % (g, d),
                     ring_send.at[g, d, 3, rows],
                     ring_in.at[g, d, 3, rows],
-                    (up, down)[d],
+                    (up2, down2)[d] if g in early else (up, down)[d],
                 )
             return
         for d in (0, 1):
             value = term(g, st if d == 0 else -st)
-            if st == 3:
+            joins = 2 if g in early else 3
+            if st < joins:
+                arrived("r%d%d%d" % (g, d, st + 1), ring_in.at[g, d, st])
+                value = value + ring_in[g, d, st].astype(F32)
+            if st == joins:
                 rows, rest = rows_of(d), rows_of(1 - d)
+                if g in early:
+                    arrived("r%d%d3" % (g, d), ring_in.at[g, d, 2])
+                    value = value + ring_in[g, d, 2].astype(F32)
                 arrived("r%d%d4" % (g, d), ring_in.at[g, d, 3, rows])
-                ring_send[g, d, 2, rows, :] = (
+                ring_send[g, d, st - 1, rows, :] = (
                     value[HALF * d : HALF * (d + 1)] + ring_in[g, d, 3, rows, :].astype(F32)
                 ).astype(BF16)
-                ring_send[g, d, 2, rest, :] = value[HALF * (1 - d) : HALF * (2 - d)].astype(BF16)
+                ring_send[g, d, st - 1, rest, :] = value[HALF * (1 - d) : HALF * (2 - d)].astype(BF16)
             else:
-                arrived("r%d%d%d" % (g, d, st + 1), ring_in.at[g, d, st])
-                ring_send[g, d, st - 1] = (value + ring_in[g, d, st].astype(F32)).astype(BF16)
+                ring_send[g, d, st - 1] = value.astype(BF16)
             send(
                 "r%d%d%d" % (g, d, st),
                 ring_send.at[g, d, st - 1],
@@ -583,42 +593,42 @@
         arrived("npc%d" % d, npair.at[(m_core - 2 * d + 8) % 8])
     rows_sum(False, 0)
     stage(0, 4)
+    rows_sum(True, 0)
+    stage(0, 3)
     terms_sum(0)
 
+    rows_sum(False, 1, 2)
     terms(1, False, ht_send)
     send("ht1", ht_send.at[1], ht_sib.at[1], sibling)
     terms(1, True, ht_own)
-    rows_sum(True, 0)
-    rows_sum(False, 1, 2)
     stage(2, 4)
     rows_sum(False, 3)
     stage(1, 4)
+    stage(0, 2)
+    rows_sum(True, 1, 2)
     for d in (0, 1, 2, 3):
         arrived("bpc%d" % d, bpair.at[bp_index(y, yh, (x + 4 - d) % 4, 1 - core)])
     stage(3, 4)
-    stage(0, 3)
-    rows_sum(True, 1, 2)
     stage(2, 3)
     stage(1, 3)
     rows_sum(True, 3)
+    stage(3, 3)
+    stage(0, 1)
     terms_sum(1)
-    stage(3, 3)
-    stage(0, 2)
     stage(2, 2)
     stage(1, 2)
+    stage(3, 2)
+    finish(0)
     y_send[...] = x_sum(0).astype(BF16)
     send("by", y_send, y_in, y_far)
-    stage(3, 2)
-    stage(0, 1)
     stage(2, 1)
     stage(1, 1)
     stage(3, 1)
-    finish(0)
     finish(2)
     finish(1)
+    finish(3)
+
     near = x_sum(1)
-    finish(3)
-
     arrived("by", y_in)
     branch = (near + y_in[...].astype(F32)).astype(BF16)
     sample_ref[...] = (branch.astype(F32) + noise_level * noise_ref[...].astype(F32)).astype(BF16)

time: 73.1 us -> 71.8 us (0.982)
    pallas_call x1, Pallas kernels: 70.7 us -> 69.9 us  [shards(): pl.pallas_call(kernel, out_shape=tuple((pltpu.VMEM(out.shape, out.dtype)...]
where the time goes in v7:
time: 71.8 us; the launch traced here: 71.6 us
  Pallas kernels  70.8 us (99%)
  between operations  0.8 us (1%)
    pallas_call x1, Pallas kernels, shards(): pl.pallas_call(kernel, out_shape=tuple((pltpu.VMEM(out.shape, out.dtype)...  69.9 us

profile of v7, /device:TPU:2, one launch (start us, length us, event | category | flops | bytes accessed | tf_op | source)
XLA Modules:
  0.0 71.6 jit_solution(6327530108082426416)
XLA Ops:
  0.6 69.9 %shard_map.94 = (bf16[192,384]{1,0:T(8,128)(2,1)S(1)}, f32[192,384]{1,0:T(8,128)S(1)}, f32[192,128]{1,0:T(8,128)S(1)}) custom-call(bf16[384,3072]{1,0:T(8,128)(2,1)} %hidden_hbm.1, bf16[192,384]{1,0:T(8,128)(2,1)} %bitcast.4, f32[1,3072]{1,0:T(1,128)} %bitcast.5, f32[2,128]{1,0:T(2,128)} %qk_gain_hbm.1, bf16[192,384]{1,0:T(8,128)(2,1)} %wq_hbm.1, ...), custom_call_target="tpu_custom_call" | custom-call | tf_op jit(solution)/shard_map/pallas_call | solution.py:710
  70.6 0.8 %shard_map.95 = (bf16[192,384]{1,0:T(8,128)(2,1)}, f32[192,384]{1,0:T(8,128)}, f32[192,128]{1,0:T(8,128)}) custom-call(bf16[192,384]{1,0:T(8,128)(2,1)S(1)} %get-tuple-element.9.a_ref, f32[192,384]{1,0:T(8,128)S(1)} %get-tuple-element.10.b_ref, f32[192,128]{1,0:T(8,128)S(1)} %get-tuple-element.11.c_ref), custom_call_target="tpu_custom_call" | custom-call | tf_op jit(solution)/shard_map/pallas_call | solution.py:728

commit v8 on v7

--- a/solution.py
+++ b/solution.py
@@ -417,9 +417,11 @@
         chunk = bpair.at[bp_index(y, yh, (x + 4 - d) % 4, core)]
         arrived("bp%d" % d, chunk)
         send("bpc%d" % d, chunk, chunk, sibling)
+    halo_send("dout", dout_t, dout_at, 1)
     halo_wait("k", k_at)
     peak = jnp.maximum(peak, scores(0))
     peak = jnp.maximum(peak, scores(2))
+    halo_send("q", q_t, q_at, 1)
     total = jnp.zeros((1, TOK), F32)
     for col in range(3):
         value = jnp.exp(exps[col] - peak)
@@ -432,12 +434,10 @@
         value = exps[col] / total
         exps[col] = value
         w_b[col] = value.astype(BF16)
-    halo_send("dout", dout_t, dout_at, 1)
     halo_wait("v", v_at)
     attended = dot(kv[0, 1], w_b[0]) + dot(kv[1, 1], w_b[1]) + dot(kv[2, 1], w_b[2])
     g_own[3] = attended.astype(BF16)
 
-    halo_send("q", q_t, q_at, 1)
     def terms(phase, own, buf):
         h = 1 - yh if phase == 0 else yh
         c = core if own else 1 - core
@@ -567,15 +567,16 @@
     terms(0, True, ht_own)
     halo_wait("dout", dout_at)
     halo_wait("q", q_at)
-    halo_wait("stats", stats_at)
     keys = kv[1, 0].T
     values = kv[1, 1].T
     dk = dot_t(q_t[...], ds_b[1])
     dv = dot_t(dout_t[...], w_b[1])
     for side in (0, 1):
-        score = dot(keys, q_in[side]) * head_scale
-        exps[side] = jnp.exp(score - stats_in[side, 0, 0:1, :]) / stats_in[side, 1, 0:1, :]
+        exps[side] = dot(keys, q_in[side]) * head_scale
         wgs[side] = dot(values, dout_in[side])
+    halo_wait("stats", stats_at)
+    for side in (0, 1):
+        exps[side] = jnp.exp(exps[side] - stats_in[side, 0, 0:1, :]) / stats_in[side, 1, 0:1, :]
     for side in (0, 1):
         w_b[side] = exps[side].astype(BF16)
         dv = dv + dot_t(dout_in[side], w_b[side])

time: 71.8 us -> 72.1 us (level)
  no operation moved by 1% of the time
where the time goes in v8:
time: 72.1 us; the launch traced here: 71.1 us
  Pallas kernels  70.3 us (98%)
  between operations  0.8 us (1%)
    pallas_call x1, Pallas kernels, shards(): pl.pallas_call(kernel, out_shape=tuple((pltpu.VMEM(out.shape, out.dtype)...  69.5 us

profile of v8, /device:TPU:2, one launch (start us, length us, event | category | flops | bytes accessed | tf_op | source)
XLA Modules:
  0.0 71.1 jit_solution(10901784272513465281)
XLA Ops:
  0.6 69.5 %shard_map.94 = (bf16[192,384]{1,0:T(8,128)(2,1)S(1)}, f32[192,384]{1,0:T(8,128)S(1)}, f32[192,128]{1,0:T(8,128)S(1)}) custom-call(bf16[384,3072]{1,0:T(8,128)(2,1)} %hidden_hbm.1, bf16[192,384]{1,0:T(8,128)(2,1)} %bitcast.4, f32[1,3072]{1,0:T(1,128)} %bitcast.5, f32[2,128]{1,0:T(2,128)} %qk_gain_hbm.1, bf16[192,384]{1,0:T(8,128)(2,1)} %wq_hbm.1, ...), custom_call_target="tpu_custom_call" | custom-call | tf_op jit(solution)/shard_map/pallas_call | solution.py:711
  70.2 0.8 %shard_map.95 = (bf16[192,384]{1,0:T(8,128)(2,1)}, f32[192,384]{1,0:T(8,128)}, f32[192,128]{1,0:T(8,128)}) custom-call(bf16[192,384]{1,0:T(8,128)(2,1)S(1)} %get-tuple-element.9.a_ref, f32[192,384]{1,0:T(8,128)S(1)} %get-tuple-element.10.b_ref, f32[192,128]{1,0:T(8,128)S(1)} %get-tuple-element.11.c_ref), custom_call_target="tpu_custom_call" | custom-call | tf_op jit(solution)/shard_map/pallas_call | solution.py:729

commit v9 on v7

--- a/solution.py
+++ b/solution.py
@@ -565,6 +565,9 @@
     terms(0, False, ht_send)
     send("ht0", ht_send.at[0], ht_sib.at[0], sibling)
     terms(0, True, ht_own)
+    terms(1, False, ht_send)
+    send("ht1", ht_send.at[1], ht_sib.at[1], sibling)
+    terms(1, True, ht_own)
     halo_wait("dout", dout_at)
     halo_wait("q", q_at)
     halo_wait("stats", stats_at)
@@ -598,9 +601,6 @@
     terms_sum(0)
 
     rows_sum(False, 1, 2)
-    terms(1, False, ht_send)
-    send("ht1", ht_send.at[1], ht_sib.at[1], sibling)
-    terms(1, True, ht_own)
     stage(2, 4)
     rows_sum(False, 3)
     stage(1, 4)

time: 71.8 us -> 71.8 us (level)
  no operation moved by 1% of the time
where the time goes in v9:
time: 71.8 us; the launch traced here: 71.6 us
  Pallas kernels  70.8 us (99%)
  between operations  0.8 us (1%)
    pallas_call x1, Pallas kernels, shards(): pl.pallas_call(kernel, out_shape=tuple((pltpu.VMEM(out.shape, out.dtype)...  70 us

profile of v9, /device:TPU:2, one launch (start us, length us, event | category | flops | bytes accessed | tf_op | source)
XLA Modules:
  0.0 71.6 jit_solution(5344019587539827797)
XLA Ops:
  0.6 70.0 %shard_map.94 = (bf16[192,384]{1,0:T(8,128)(2,1)S(1)}, f32[192,384]{1,0:T(8,128)S(1)}, f32[192,128]{1,0:T(8,128)S(1)}) custom-call(bf16[384,3072]{1,0:T(8,128)(2,1)} %hidden_hbm.1, bf16[192,384]{1,0:T(8,128)(2,1)} %bitcast.4, f32[1,3072]{1,0:T(1,128)} %bitcast.5, f32[2,128]{1,0:T(2,128)} %qk_gain_hbm.1, bf16[192,384]{1,0:T(8,128)(2,1)} %wq_hbm.1, ...), custom_call_target="tpu_custom_call" | custom-call | tf_op jit(solution)/shard_map/pallas_call | solution.py:710
  70.6 0.8 %shard_map.95 = (bf16[192,384]{1,0:T(8,128)(2,1)}, f32[192,384]{1,0:T(8,128)}, f32[192,128]{1,0:T(8,128)}) custom-call(bf16[192,384]{1,0:T(8,128)(2,1)S(1)} %get-tuple-element.9.a_ref, f32[192,384]{1,0:T(8,128)S(1)} %get-tuple-element.10.b_ref, f32[192,128]{1,0:T(8,128)S(1)} %get-tuple-element.11.c_ref), custom_call_target="tpu_custom_call" | custom-call | tf_op jit(solution)/shard_map/pallas_call | solution.py:728
